TPU v7x, 512 devices: a whole 4x8x8 slice. The times are simulated.
512 devices in a mesh: blk: 128 (over z, y, core), rep: 4 (over x).
Axes of the slice: x: 4, y: 8, z: 8, core: 2. Of those that a mesh axis runs over, the one named last changes fastest.
Arguments:
- pair_blocks: bfloat16 [128, 128, 128, 128], P('blk', 'rep'), may hold values from -6 to 6
- kept_pairs: int32 [128, 2], replicated, may hold values from 0 to 63, as said below
- owner: int32 [64, 64], replicated, may hold values from -1 to 127, as said below
- norm_gain: float32 [128], replicated, may hold values from 0.5 to 1.5
- norm_offset: float32 [128], replicated, may hold values from -3 to 3
- w_query: bfloat16 [128, 128], replicated
- w_key: bfloat16 [128, 128], replicated
- w_value: bfloat16 [128, 128], replicated, may hold values from -0.5 to 0.5
- w_gate: bfloat16 [128, 128], replicated, may hold values from -0.5 to 0.5
- gate_bias: float32 [128], replicated, may hold values from -4 to 4
- w_bias: bfloat16 [128, 4], replicated, may hold values from -1 to 1
- w_out: bfloat16 [128, 128], replicated, may hold values from -0.5 to 0.5
Outputs:
- update: bfloat16 [128, 128, 128, 128], P('blk', 'rep')
Inputs may be any that keep to these rules, and one draw needn't show every extreme that they name: `kept_pairs`: rows sorted by block row, then block column; no pair twice; every block row I keeps its diagonal block (I, I) and 1 to 3 blocks in all, some row exactly 3; a row of 2 or more blocks keeps column (I + 32) mod 64; block row I + 32 keeps the columns of block row I shifted by 64 / 2 modulo 64. owner[I, J] is the row of kept_pairs holding (I, J), -1 where the block is not kept.
All inputs are finite; a program needn't handle non-finite values.
Results may differ from a plain program's by a relative error of at most 0.011.
Values may be sent and summed in bfloat16 or wider, within the bound.
A program may use at most 64 MiB of HBM per device.

v0:
```python
import jax
import jax.numpy as jnp
from jax import lax
from jax.sharding import PartitionSpec as P

ROW_MOST = 3


def shifted(value, axis, steps):
    count = lax.axis_size(axis)
    initial, last = (max(0, -steps), min(count, count - steps))
    return lax.ppermute(value, axis, [(source, source + steps) for source in range(initial, last)])


def norm_rows(pairs, gain, offset):
    values = pairs.astype(jnp.float32)
    center = jnp.mean(values, axis=-1, keepdims=True)
    spread = jnp.mean((values - center) ** 2, axis=-1, keepdims=True)
    return ((values - center) * lax.rsqrt(spread + 1e-05) * gain + offset).astype(jnp.bfloat16)


def project(feats, weight):
    flat = feats.reshape(-1, feats.shape[-1])
    result = jnp.dot(flat, weight, preferred_element_type=jnp.float32)
    return result.reshape(feats.shape[:-1] + (weight.shape[1],))


def per_device(
    pair_blocks,
    kept_pairs,
    owner,
    norm_gain,
    norm_offset,
    w_query,
    w_key,
    w_value,
    w_gate,
    gate_bias,
    w_bias,
    w_out,
):
    rows = pair_blocks.shape[1]
    width = pair_blocks.shape[2]
    heads = w_bias.shape[1]
    inner = w_query.shape[1]
    head_size = inner // heads
    kept = kept_pairs.shape[0]
    normed = norm_rows(pair_blocks[0], norm_gain, norm_offset)
    query = (
        (project(normed, w_query) * head_size ** (-0.5))
        .astype(jnp.bfloat16)
        .reshape(rows, width, heads, head_size)
    )
    key_own = project(normed, w_key).astype(jnp.bfloat16)
    value_own = project(normed, w_value).astype(jnp.bfloat16)
    gate = jax.nn.sigmoid(project(normed, w_gate) + gate_bias)
    bias_piece = project(normed, w_bias).astype(jnp.bfloat16).transpose(2, 0, 1)
    all_bias = lax.all_gather(bias_piece[None], "blk", axis=0, tiled=True)
    device = lax.axis_index("blk")
    row_i = kept_pairs[device, 0]
    col_j = kept_pairs[device, 1]
    offsets = [0]
    for step in range(1, ROW_MOST):
        offsets = offsets + [step, -step]
    candidates = []
    valid_list = []
    bias_slots = []
    for offset in offsets:
        if offset == 0:
            member = (key_own, value_own)
        else:
            member = shifted((key_own, value_own), "blk", offset)
        slot = device - offset
        safe = jnp.clip(slot, 0, kept - 1)
        valid = (slot >= 0) & (slot < kept) & (kept_pairs[safe, 0] == row_i)
        candidates.append(member)
        valid_list.append(valid)
        bias_slots.append(owner[col_j, kept_pairs[safe, 1]])
    slot_array = jnp.stack(bias_slots)
    chosen = all_bias[jnp.clip(slot_array, 0, kept - 1)]
    chosen = jnp.where((slot_array >= 0)[:, None, None, None], chosen, jnp.zeros((), jnp.bfloat16))
    full_bias = lax.all_gather(chosen, "rep", axis=2, tiled=True)

    def update_state(state, keys, values, bias):
        top, total, accum = state
        keys4 = keys.reshape(rows, width, heads, head_size)
        values4 = values.reshape(rows, width, heads, head_size)
        scores = jnp.einsum("ijhd,ikhd->hijk", query, keys4, preferred_element_type=jnp.float32)
        scores = scores + bias[:, None].astype(jnp.float32)
        new_top = jnp.maximum(top, jnp.max(scores, axis=-1))
        factor = jnp.exp(top - new_top)
        weights = jnp.exp(scores - new_top[..., None])
        total = total * factor + jnp.sum(weights, axis=-1)
        product = jnp.einsum(
            "hijk,ikhd->ijhd",
            weights.astype(jnp.bfloat16),
            values4,
            preferred_element_type=jnp.float32,
        )
        accum = accum * factor.transpose(1, 2, 0)[..., None] + product
        return (new_top, total, accum)

    state = (
        jnp.full((heads, rows, width), -1e30, jnp.float32),
        jnp.zeros((heads, rows, width), jnp.float32),
        jnp.zeros((rows, width, heads, head_size), jnp.float32),
    )
    for place in range(len(offsets)):
        keys, values = candidates[place]
        bias = full_bias[place]
        state = lax.cond(
            valid_list[place],
            lambda current: update_state(current, keys, values, bias),
            lambda current: current,
            state,
        )
    top, total, accum = state
    attended = accum / total.transpose(1, 2, 0)[..., None]
    gated = (gate * attended.reshape(rows, width, inner)).astype(jnp.bfloat16)
    return project(gated, w_out).astype(jnp.bfloat16)[None]


def solution(mesh):
    return jax.shard_map(
        per_device,
        mesh=mesh,
        in_specs=(
            P("blk", "rep", None, None),
            P(),
            P(),
            P(),
            P(),
            P(),
            P(),
            P(),
            P(),
            P(),
            P(),
            P(),
        ),
        out_specs=P("blk", "rep", None, None),
        check_vma=False,
    )
```

profile of v0, /device:TPU:54, one launch (start us, length us, event | category | flops | bytes accessed | tf_op | source)
XLA Modules:
  0.0 215.3 jit_solution(7438602052403149718)
XLA Ops:
  19.5 2.7 %collective-permute-start.1 = (bf16[32,128,128]{2,1,0:T(8,128)(2,1)}, bf16[32,128,128]{2,1,0:T(8,128)(2,1)}, u32[]{:S(2)}, u32[]{:S(2)}) collective-permute-start(bf16[32,128,128]{2,1,0:T(8,128)(2,1)} %convolution_convert_fusion), channel_id=1, source_target_pairs={{0,4},{4,8},{8,12},{12,16},{16,20},{20,24},{24,28},{28,32},{32,36}... | collective-permute-start | bytes 3145736 | tf_op jit(solution)/shard_map/ppermute | solution.py:12
  22.2 2.9 %collective-permute-start.2 = (bf16[32,128,128]{2,1,0:T(8,128)(2,1)}, bf16[32,128,128]{2,1,0:T(8,128)(2,1)S(1)}, u32[]{:S(2)}, u32[]{:S(2)}) collective-permute-start(bf16[32,128,128]{2,1,0:T(8,128)(2,1)} %convolution_convert_fusion.1), channel_id=1, source_target_pairs={{4,0},{8,4},{12,8},{16,12},{20,16},{24,20},{28,24},{32,28},{36,32}... | collective-permute-start | bytes 3145736 | tf_op jit(solution)/shard_map/ppermute | solution.py:12
  25.0 2.4 %collective-permute-start.3 = (bf16[32,128,128]{2,1,0:T(8,128)(2,1)}, bf16[32,128,128]{2,1,0:T(8,128)(2,1)}, u32[]{:S(2)}, u32[]{:S(2)}) collective-permute-start(bf16[32,128,128]{2,1,0:T(8,128)(2,1)} %convolution_convert_fusion), channel_id=1, source_target_pairs={{4,0},{8,4},{12,8},{16,12},{20,16},{24,20},{28,24},{32,28},{36,32}... | collective-permute-start | bytes 3145736 | tf_op jit(solution)/shard_map/ppermute | solution.py:12
  27.5 2.6 %collective-permute-start.4 = (bf16[32,128,128]{2,1,0:T(8,128)(2,1)}, bf16[32,128,128]{2,1,0:T(8,128)(2,1)}, u32[]{:S(2)}, u32[]{:S(2)}) collective-permute-start(bf16[32,128,128]{2,1,0:T(8,128)(2,1)} %convolution_convert_fusion.1), channel_id=1, source_target_pairs={{0,8},{4,12},{8,16},{12,20},{16,24},{20,28},{24,32},{28,36},{32,40... | collective-permute-start | bytes 3145736 | tf_op jit(solution)/shard_map/ppermute | solution.py:12
  43.6 3.1 %stack.21 = s32[5,1]{1,0:T(8,128)S(1)} concatenate(s32[1,1]{1,0:T(1,128)} %get-tuple-element.317, s32[1,1]{1,0:T(1,128)} %get-tuple-element.316, s32[1,1]{1,0:T(1,128)} %get-tuple-element.315, s32[1,1]{1,0:T(1,128)} %get-tuple-element.318, s32[1,1]{1,0:T(1,128)} %get-tuple-element.314), dimensions={0} | concatenate | bytes 40 | tf_op jit(solution)/shard_map/stack | solution.py:79
  46.7 3.2 %stack.20 = s32[5]{0:T(128)S(1)} concatenate(s32[1]{0:T(128)} %bitcast.37, s32[1]{0:T(128)} %bitcast.39, s32[1]{0:T(128)} %bitcast.41, s32[1]{0:T(128)} %bitcast.43, s32[1]{0:T(128)} %bitcast.45), dimensions={0} | concatenate | bytes 40 | tf_op jit(solution)/shard_map/stack | solution.py:79
  50.1 5.6 %collective-permute-start.5 = (bf16[32,128,128]{2,1,0:T(8,128)(2,1)}, bf16[32,128,128]{2,1,0:T(8,128)(2,1)}, u32[]{:S(2)}, u32[]{:S(2)}) collective-permute-start(bf16[32,128,128]{2,1,0:T(8,128)(2,1)} %convolution_convert_fusion), channel_id=1, source_target_pairs={{0,8},{4,12},{8,16},{12,20},{16,24},{20,28},{24,32},{28,36},{32,40... | collective-permute-start | bytes 3145736 | tf_op jit(solution)/shard_map/ppermute | solution.py:12
  57.6 2.6 %collective-permute-start.7 = (bf16[32,128,128]{2,1,0:T(8,128)(2,1)}, bf16[32,128,128]{2,1,0:T(8,128)(2,1)}, u32[]{:S(2)}, u32[]{:S(2)}) collective-permute-start(bf16[32,128,128]{2,1,0:T(8,128)(2,1)} %convolution_convert_fusion), channel_id=1, source_target_pairs={{8,0},{12,4},{16,8},{20,12},{24,16},{28,20},{32,24},{36,28},{40,32... | collective-permute-start | bytes 3145736 | tf_op jit(solution)/shard_map/ppermute | solution.py:12
  68.4 65.0 %all-gather.3.cloned.1.call-done = bf16[512,32,128]{2,1,0:T(8,128)(2,1)} async-done(((bf16[4,32,128]{2,1,0:T(8,128)(2,1)}), bf16[512,32,128]{2,1,0:T(8,128)(2,1)}) %all-gather.3.cloned.1.call-update) | async-done | bytes 4194320 | tf_op jit(solution)/shard_map/all_gather | solution.py:58
  133.4 2.8 %gather_fusion = bf16[5,4,32,128]{3,2,1,0:T(8,128)(2,1)S(1)} fusion(bf16[128,4,32,128]{3,2,1,0:T(8,128)(2,1)} %bitcast.136, s32[1024]{0:T(1024)S(1)} %pad_clamp_fusion), kind=kCustom, calls=%fused_computation | custom fusion | bytes 327700 | tf_op jit(solution)/shard_map/gather | solution.py:80
  136.3 14.0 %all_gather.7 = bf16[5,4,128,128]{3,2,1,0:T(8,128)(2,1)S(1)} all-gather(bf16[5,4,32,128]{3,2,1,0:T(8,128)(2,1)S(1)} %broadcast_select_fusion), channel_id=1, replica_groups=mesh['blk'=128,'rep'=4] {'rep'}, dimensions={2}, use_global_device_ids=true | all-gather | bytes 819200 | tf_op jit(solution)/shard_map/all_gather | solution.py:82
  151.1 12.8 %conditional.5 = (f32[4,32,128]{2,1,0:T(8,128)S(1)}, f32[4,32,128]{2,1,0:T(8,128)S(1)}, f32[32,128,4,32]{1,3,2,0:T(8,128)S(1)}) conditional(s32[]{:T(128)} %convert_element_type.135, () %tuple.38, (bf16[32,128,128]{2,1,0:T(8,128)(2,1)}, bf16[32,128,4,32]{1,3,2,0:T(8,128)(2,1)S(1)}, bf16[1,4,128,128]{3,2,1,0:T(8,128)(2,1)S(1)}, ...), branch_computations={%region_2.3_spmd, %region_3.6_spmd} | conditional | flops 281673728 | bytes 37093456 | solution.py:111
  154.4 3.4 %fusion = (bf16[4,32,128,128]{2,3,1,0:T(8,128)(2,1)}, f32[4,32,128]{2,1,0:T(8,128)S(1)}) fusion(f32[4,32,128,128]{2,3,1,0:T(8,128)S(1)} %get-tuple-element.310, f32[4,32,128]{2,1,0:T(8,128)S(1)} %get-tuple-element.334, f32[4,128,128]{1,2,0:T(8,128)S(1)} %bitcast_convert_fusion), kind=kLoop, calls=%fused_computation.3 | loop fusion | flops 8372224 | bytes 12976128 | tf_op jit(solution)/shard_map/cond/branch_1_fun/convert_element_type | solution.py:96
  160.2 3.7 %bitcast_add_fusion = f32[32,128,4,32]{1,3,2,0:T(8,128)S(1)} fusion(bf16[32,128,4,32]{1,3,2,0:T(8,128)(2,1)} %bitcast.129, bf16[4,32,128,128]{2,3,1,0:T(8,128)(2,1)} %get-tuple-element.307, f32[32,128,4]{1,2,0:T(4,128)S(1)} %copy.120), kind=kOutput, calls=%fused_computation.7 | convolution fusion | flops 134742016 | bytes 7405568 | tf_op jit(solution)/shard_map/cond/branch_1_fun/hijk,ikhd->ijhd/dot_general | solution.py:94
  164.0 17.0 %conditional.6 = ((f32[4,32,128]{2,1,0:T(8,128)S(1)}, f32[4,32,128]{2,1,0:T(8,128)S(1)}, f32[32,128,4,32]{1,3,2,0:T(8,128)S(1)})) conditional(s32[]{:T(128)} %convert_element_type.134, (f32[4,32,128]{2,1,0:T(8,128)S(1)}, f32[4,32,128]{2,1,0:T(8,128)S(1)}, f32[32,128,4,32]{1,3,2,0:T(8,128)S(1)}) %conditional.5, (bf16[32,128,128]{2,1,0:T(8,128)(2,1)}, ...), branch_computations={%region_6.7_spmd, %region_7.10_spmd} | conditional | flops 282181632 | bytes 39256124 | solution.py:111
  168.1 2.7 %add_reduce_fusion.1 = (f32[4,32,128]{2,1,0:T(8,128)S(1)}, f32[4,32,128,128]{2,3,1,0:T(8,128)S(1)}) fusion(f32[4,128,128]{1,2,0:T(8,128)S(1)} %bitcast_convert_fusion.1, bf16[32,128,4,32]{1,3,2,0:T(8,128)(2,1)} %bitcast.131, bf16[32,128,4,32]{1,3,2,0:T(8,128)(2,1)S(1)} %get-tuple-element.254), kind=kOutput, calls=%fused_computation.17 | convolution fusion | flops 138395648 | bytes 10813440 | tf_op jit(solution)/shard_map/cond/branch_1_fun/ijhd,ikhd->hijk/dot_general | solution.py:88
  171.5 3.4 %fusion.11 = (bf16[4,32,128,128]{2,3,1,0:T(8,128)(2,1)}, f32[4,32,128]{2,1,0:T(8,128)S(1)}) fusion(f32[4,32,128,128]{2,3,1,0:T(8,128)S(1)} %get-tuple-element.294, f32[4,32,128]{2,1,0:T(8,128)S(1)} %get-tuple-element.340, f32[4,128,128]{1,2,0:T(8,128)S(1)} %bitcast_convert_fusion.1), kind=kLoop, calls=%fused_computation.18 | loop fusion | flops 8372224 | bytes 12976128 | tf_op jit(solution)/shard_map/cond/branch_1_fun/convert_element_type | solution.py:96
  177.3 3.7 %bitcast_add_fusion.1 = f32[32,128,4,32]{1,3,2,0:T(8,128)S(1)} fusion(f32[32,128,4,32]{1,3,2,0:T(8,128)S(1)} %get-tuple-element.102, bf16[32,128,4,32]{1,3,2,0:T(8,128)(2,1)} %bitcast.125, bf16[4,32,128,128]{2,3,1,0:T(8,128)(2,1)} %get-tuple-element.291, f32[32,128,4]{1,2,0:T(4,128)S(1)} %copy.123), kind=kOutput, calls=%fused_computation.22 | convolution fusion | flops 135266304 | bytes 9502720 | tf_op jit(solution)/shard_map/cond/branch_1_fun/hijk,ikhd->ijhd/dot_general | solution.py:94
  181.0 18.5 %conditional.8 = ((f32[4,32,128]{2,1,0:T(8,128)S(1)}, f32[4,32,128]{2,1,0:T(8,128)S(1)}, f32[32,128,4,32]{1,3,2,0:T(8,128)S(1)})) conditional(s32[]{:T(128)} %convert_element_type.132, (f32[4,32,128]{2,1,0:T(8,128)S(1)}, f32[4,32,128]{2,1,0:T(8,128)S(1)}, f32[32,128,4,32]{1,3,2,0:T(8,128)S(1)}) %get-tuple-element.360, ...), branch_computations={%region_14.15_spmd, %region_15.18_spmd} | conditional | flops 282181632 | bytes 40304700 | solution.py:111
  186.7 2.7 %add_reduce_fusion.3 = (f32[4,32,128]{2,1,0:T(8,128)S(1)}, f32[4,32,128,128]{2,3,1,0:T(8,128)S(1)}) fusion(f32[4,128,128]{1,2,0:T(8,128)S(1)} %fusion.40, bf16[32,128,4,32]{1,3,2,0:T(8,128)(2,1)} %bitcast.133, bf16[32,128,4,32]{1,3,2,0:T(8,128)(2,1)S(1)} %get-tuple-element.268), kind=kOutput, calls=%fused_computation.45 | convolution fusion | flops 138395648 | bytes 10813440 | tf_op jit(solution)/shard_map/cond/branch_1_fun/ijhd,ikhd->hijk/dot_general | solution.py:88
  190.1 3.4 %fusion.31 = (bf16[4,32,128,128]{2,3,1,0:T(8,128)(2,1)}, f32[4,32,128]{2,1,0:T(8,128)S(1)}) fusion(f32[4,32,128,128]{2,3,1,0:T(8,128)S(1)} %get-tuple-element.302, f32[4,32,128]{2,1,0:T(8,128)S(1)} %get-tuple-element.352, f32[4,128,128]{1,2,0:T(8,128)S(1)} %fusion.40), kind=kLoop, calls=%fused_computation.46 | loop fusion | flops 8372224 | bytes 12976128 | tf_op jit(solution)/shard_map/cond/branch_1_fun/convert_element_type | solution.py:96
  195.8 3.7 %bitcast_add_fusion.3 = f32[32,128,4,32]{1,3,2,0:T(8,128)S(1)} fusion(f32[32,128,4,32]{1,3,2,0:T(8,128)S(1)} %get-tuple-element.116, bf16[32,128,4,32]{1,3,2,0:T(8,128)(2,1)} %bitcast.127, bf16[4,32,128,128]{2,3,1,0:T(8,128)(2,1)} %get-tuple-element.299, f32[32,128,4]{1,2,0:T(4,128)S(1)} %copy.129), kind=kOutput, calls=%fused_computation.50 | convolution fusion | flops 135266304 | bytes 9502720 | tf_op jit(solution)/shard_map/cond/branch_1_fun/hijk,ikhd->ijhd/dot_general | solution.py:94
  201.4 3.0 %copy.157 = f32[32,128,128]{2,1,0:T(8,128)} copy(f32[32,128,128]{1,2,0:T(8,128)} %bitcast.124) | data formatting | bytes 4194304 | tf_op jit(solution)/shard_map/reshape | solution.py:119
  204.4 4.0 %fusion.62 = bf16[1,32,128,128]{3,2,1,0:T(8,128)(2,1)} fusion(f32[32,128,128]{2,1,0:T(8,128)} %copy.157, f32[128]{0:T(128)S(1)} %copy-done.24, bf16[128,128]{1,0:T(8,128)(2,1)S(1)} %copy-done.17, bf16[128,128]{1,0:T(8,128)(2,1)S(1)} %copy-done.18, bf16[1,32,128,128]{3,2,1,0:T(8,128)(2,1)S(1)} %copy-done.6, f32[128]{0:T(128)S(1)} %copy-done.21, ...), kind=kOutput, calls=%fused_computation.89 | convolution fusion | flops 275251200 | bytes 4294144 | tf_op jit(solution)/shard_map/dot_general | solution.py:24
  (102 shorter events, 42.7 us)
Async XLA Ops:
  6.5 6.3 %copy-start = (bf16[128,128]{1,0:T(8,128)(2,1)S(1)}, bf16[128,128]{1,0:T(8,128)(2,1)}, u32[]{:S(2)}) copy-start(bf16[128,128]{1,0:T(8,128)(2,1)} %param.28) | copy-start | bytes 98308
  6.5 4.1 %copy-start.5 = (bf16[1,32,128,128]{3,2,1,0:T(8,128)(2,1)S(1)}, bf16[1,32,128,128]{3,2,1,0:T(8,128)(2,1)}, u32[]{:S(2)}) copy-start(bf16[1,32,128,128]{3,2,1,0:T(8,128)(2,1)} %param.22) | copy-start | bytes 3145732
  6.5 4.1 %copy-start.20 = (f32[128]{0:T(128)S(1)}, f32[128]{0:T(128)}, u32[]{:S(2)}) copy-start(f32[128]{0:T(128)} %param.26) | copy-start | bytes 1540
  6.5 4.1 %copy-start.22 = (f32[128]{0:T(128)S(1)}, f32[128]{0:T(128)}, u32[]{:S(2)}) copy-start(f32[128]{0:T(128)} %param.25) | copy-start | bytes 1540
  6.5 4.1 %copy-start.19 = (bf16[128,4]{0,1:T(4,128)(2,1)S(1)}, bf16[128,4]{0,1:T(4,128)(2,1)}, u32[]{:S(2)}) copy-start(bf16[128,4]{0,1:T(4,128)(2,1)} %param.32) | copy-start | bytes 3076
  6.5 126.8 %all-gather.3.cloned.1.call-start = ((), (), s32[]{:S(2)}) async-start(), calls=%async_computation | async-start | bytes 4227072 | tf_op jit(solution)/shard_map/all_gather | solution.py:58
  10.7 56.0 %copy-start.13 = (f32[32,128]{1,0:T(8,128)}, f32[32,128]{1,0:T(8,128)S(1)}, u32[]{:S(2)}) copy-start(f32[32,128]{1,0:T(8,128)S(1)} %add_rsqrt_fusion) | copy-start | bytes 49156
  12.1 5.0 %copy-start.15 = (bf16[128,128]{1,0:T(8,128)(2,1)S(1)}, bf16[128,128]{1,0:T(8,128)(2,1)}, u32[]{:S(2)}) copy-start(bf16[128,128]{1,0:T(8,128)(2,1)} %param.29) | copy-start | bytes 98308
  15.1 15.0 %copy-start.12 = (s32[128,2]{0,1:T(2,128)S(1)}, s32[128,2]{0,1:T(2,128)}, u32[]{:S(2)}) copy-start(s32[128,2]{0,1:T(2,128)} %param.23) | copy-start | bytes 3076
  15.1 51.6 %copy-start.16 = (bf16[128,128]{1,0:T(8,128)(2,1)S(1)}, bf16[128,128]{1,0:T(8,128)(2,1)}, u32[]{:S(2)}) copy-start(bf16[128,128]{1,0:T(8,128)(2,1)} %param.27) | copy-start | bytes 98308
  15.1 35.0 %collective-permute-start = (bf16[32,128,128]{2,1,0:T(8,128)(2,1)}, bf16[32,128,128]{2,1,0:T(8,128)(2,1)}, u32[]{:S(2)}, u32[]{:S(2)}) collective-permute-start(bf16[32,128,128]{2,1,0:T(8,128)(2,1)} %convolution_convert_fusion.1), channel_id=1, source_target_pairs={{0,4},{4,8},{8,12},{12,16},{16,20},{20,24},{24,28},{28,32},{32,36}... | collective-permute-start | bytes 3145736 | tf_op jit(solution)/shard_map/ppermute | solution.py:12
  19.5 36.2 %collective-permute-start.1 = (bf16[32,128,128]{2,1,0:T(8,128)(2,1)}, bf16[32,128,128]{2,1,0:T(8,128)(2,1)}, u32[]{:S(2)}, u32[]{:S(2)}) collective-permute-start(bf16[32,128,128]{2,1,0:T(8,128)(2,1)} %convolution_convert_fusion), channel_id=1, source_target_pairs={{0,4},{4,8},{8,12},{12,16},{16,20},{20,24},{24,28},{28,32},{32,36}... | collective-permute-start | bytes 3145736 | tf_op jit(solution)/shard_map/ppermute | solution.py:12
  22.2 35.5 %collective-permute-start.2 = (bf16[32,128,128]{2,1,0:T(8,128)(2,1)}, bf16[32,128,128]{2,1,0:T(8,128)(2,1)S(1)}, u32[]{:S(2)}, u32[]{:S(2)}) collective-permute-start(bf16[32,128,128]{2,1,0:T(8,128)(2,1)} %convolution_convert_fusion.1), channel_id=1, source_target_pairs={{4,0},{8,4},{12,8},{16,12},{20,16},{24,20},{28,24},{32,28},{36,32}... | collective-permute-start | bytes 3145736 | tf_op jit(solution)/shard_map/ppermute | solution.py:12
  25.0 156.0 %collective-permute-start.3 = (bf16[32,128,128]{2,1,0:T(8,128)(2,1)}, bf16[32,128,128]{2,1,0:T(8,128)(2,1)}, u32[]{:S(2)}, u32[]{:S(2)}) collective-permute-start(bf16[32,128,128]{2,1,0:T(8,128)(2,1)} %convolution_convert_fusion), channel_id=1, source_target_pairs={{4,0},{8,4},{12,8},{16,12},{20,16},{24,20},{28,24},{32,28},{36,32}... | collective-permute-start | bytes 3145736 | tf_op jit(solution)/shard_map/ppermute | solution.py:12
  27.5 153.6 %collective-permute-start.4 = (bf16[32,128,128]{2,1,0:T(8,128)(2,1)}, bf16[32,128,128]{2,1,0:T(8,128)(2,1)}, u32[]{:S(2)}, u32[]{:S(2)}) collective-permute-start(bf16[32,128,128]{2,1,0:T(8,128)(2,1)} %convolution_convert_fusion.1), channel_id=1, source_target_pairs={{0,8},{4,12},{8,16},{12,20},{16,24},{20,28},{24,32},{28,36},{32,40... | collective-permute-start | bytes 3145736 | tf_op jit(solution)/shard_map/ppermute | solution.py:12
  50.1 131.0 %collective-permute-start.5 = (bf16[32,128,128]{2,1,0:T(8,128)(2,1)}, bf16[32,128,128]{2,1,0:T(8,128)(2,1)}, u32[]{:S(2)}, u32[]{:S(2)}) collective-permute-start(bf16[32,128,128]{2,1,0:T(8,128)(2,1)} %convolution_convert_fusion), channel_id=1, source_target_pairs={{0,8},{4,12},{8,16},{12,20},{16,24},{20,28},{24,32},{28,36},{32,40... | collective-permute-start | bytes 3145736 | tf_op jit(solution)/shard_map/ppermute | solution.py:12
  55.7 143.9 %collective-permute-start.6 = (bf16[32,128,128]{2,1,0:T(8,128)(2,1)}, bf16[32,128,128]{2,1,0:T(8,128)(2,1)}, u32[]{:S(2)}, u32[]{:S(2)}) collective-permute-start(bf16[32,128,128]{2,1,0:T(8,128)(2,1)} %convolution_convert_fusion.1), channel_id=1, source_target_pairs={{8,0},{12,4},{16,8},{20,12},{24,16},{28,20},{32,24},{36,28},{40,32... | collective-permute-start | bytes 3145736 | tf_op jit(solution)/shard_map/ppermute | solution.py:12
  57.6 9.0 %copy-start.7 = (bf16[32,128,128]{2,1,0:T(8,128)(2,1)}, bf16[32,128,128]{2,1,0:T(8,128)(2,1)S(1)}, u32[]{:S(2)}) copy-start(bf16[32,128,128]{2,1,0:T(8,128)(2,1)S(1)} %collective-permute-done.2) | copy-start | bytes 3145732
  57.6 141.9 %collective-permute-start.7 = (bf16[32,128,128]{2,1,0:T(8,128)(2,1)}, bf16[32,128,128]{2,1,0:T(8,128)(2,1)}, u32[]{:S(2)}, u32[]{:S(2)}) collective-permute-start(bf16[32,128,128]{2,1,0:T(8,128)(2,1)} %convolution_convert_fusion), channel_id=1, source_target_pairs={{8,0},{12,4},{16,8},{20,12},{24,16},{28,20},{32,24},{36,28},{40,32... | collective-permute-start | bytes 3145736 | tf_op jit(solution)/shard_map/ppermute | solution.py:12
  154.4 3.4 %copy-start.3 = (f32[4,32,128]{2,1,0:T(8,128)}, f32[4,32,128]{2,1,0:T(8,128)S(1)}, u32[]{:S(2)}) copy-start(f32[4,32,128]{2,1,0:T(8,128)S(1)} %get-tuple-element.334) | copy-start | bytes 196612 | tf_op jit(solution)/shard_map/cond
  160.2 3.8 %copy-start.4 = (f32[4,32,128]{2,1,0:T(8,128)S(1)}, f32[4,32,128]{2,1,0:T(8,128)}, u32[]{:S(2)}) copy-start(f32[4,32,128]{2,1,0:T(8,128)} %copy-done.3) | copy-start | bytes 196612 | tf_op jit(solution)/shard_map/cond
  201.3 3.0 %copy-start.21 = (f32[128]{0:T(128)S(1)}, f32[128]{0:T(128)}, u32[]{:S(2)}) copy-start(f32[128]{0:T(128)} %param.26) | copy-start | bytes 1540
  201.4 3.0 %copy-start.23 = (f32[128]{0:T(128)S(1)}, f32[128]{0:T(128)}, u32[]{:S(2)}) copy-start(f32[128]{0:T(128)} %param.25) | copy-start | bytes 1540
  204.4 4.0 %copy-start.1 = (bf16[128,128]{1,0:T(8,128)(2,1)S(1)}, bf16[128,128]{1,0:T(8,128)(2,1)}, u32[]{:S(2)}) copy-start(bf16[128,128]{1,0:T(8,128)(2,1)} %param.28) | copy-start | bytes 98308
  (8 other events, 20.7 us)
Sparse Core Ops, SparseCore 0:
  12.9 120.4 all-gather.2
where the time goes:
time: 217 us; the launch traced here: 215 us
  waiting for transfers between devices  65 us (30%)
  local copies, waits for them, and re-layouts  32.3 us (15%)
  between operations  31.5 us (15%)
  matrix products  29.8 us (14%)
  starting transfers between devices  22.7 us (10%)
  other arithmetic  19.4 us (9%)
  blocking collectives  14 us (6%)
    all_gather x1, waiting for transfers between devices, per_device(): all_bias = lax.all_gather(bias_piece[None], 'blk', axis=0, tiled=True)  65 us
    ppermute x8, starting transfers between devices, shifted(): lax.ppermute(value, axis, [(source, source + steps) for source in range(i...  22.7 us
    another operation x9, local copies, waits for them, and re-layouts  16.1 us
    all_gather x1, blocking collectives, per_device(): full_bias = lax.all_gather(chosen, 'rep', axis=2, tiled=True)  14 us
    dot_general x5, matrix products, project(): result = jnp.dot(flat, weight, preferred_element_type=jnp.float32)  11.8 us
    dot_general x3, matrix products, update_state(): jnp.einsum('hijk,ikhd->ijhd', weights.astype(jnp.bfloat16), values4, pref...  11.2 us
    convert_element_type x3, other arithmetic, update_state(): weights.astype(jnp.bfloat16)  10.2 us
    dot_general x3, matrix products, update_state(): jnp.einsum('ijhd,ikhd->hijk', query, keys4, preferred_element_type=jnp.fl...  6.87 us
  transfers between devices with their start and end apart: 9, of which 1 were waited for; matrix products, arithmetic and copies ran while one was open for 31% of the time, Pallas kernels for 0%

commit v1 on v0

v1 whole, which is shorter than its diff:
```python
import functools

import jax
import jax.numpy as jnp
from jax import lax
from jax.experimental import pallas as pl
from jax.experimental.pallas import tpu as pltpu
from jax.sharding import PartitionSpec as P

F32 = jnp.float32
BF = jnp.bfloat16
I32 = jnp.int32
MESH = pl.DeviceIdType.MESH
LOG2E = 1.4426950408889634
MASKED = -1e30

NZ, NY, NX = 8, 8, 4
PLANE = 2 * NY
KEPT = NZ * PLANE
ROWS = 32
W = 128
HEADS, HD = 4, 32
CHUNKS = 4
RC = ROWS // CHUNKS
Y_STEPS = (1, -1, 2, -2, 3, -3, 4)
Z_STEPS = (1, -1, 2, -2, 3, -3, 4)
X_STEPS = (1, -1, 2)


def dot(a, b):
    return jnp.dot(a, b, preferred_element_type=F32)


def dot_nt(a, b):
    return lax.dot_general(a, b, (((1,), (1,)), ((), ())), preferred_element_type=F32)


def dot_tn(a, b):
    return lax.dot_general(a, b, (((0,), (0,)), ((), ())), preferred_element_type=F32)


def norm_rows(x, gain, offset):
    v = x.astype(F32)
    d = v - jnp.mean(v, axis=-1, keepdims=True)
    s = jnp.mean(d * d, axis=-1, keepdims=True)
    return (d * lax.rsqrt(s + 1e-05) * gain + offset).astype(BF)


def row_members(kept, slot):
    row = kept[slot, 0]

    def same(step):
        other = slot + step
        inside = (other >= 0) & (other < KEPT)
        return inside & (kept[jnp.clip(other, 0, KEPT - 1), 0] == row)

    m1, m2, p1, p2 = same(-1), same(-2), same(1), same(2)
    first = jnp.where(m1, -1, 1)
    second = jnp.where(m1 & p1, 1, jnp.where(m2, -2, 2))
    return first, m1 | p1, second, (m1 & p1) | m2 | p2


def bias_wants(kept, owner, slot):
    first, has_first, second, has_second = row_members(kept, slot)
    col = kept[slot, 1]
    k1 = kept[jnp.clip(slot + first, 0, KEPT - 1), 1]
    k2 = kept[jnp.clip(slot + second, 0, KEPT - 1), 1]
    g0 = owner[col, col]
    g1 = jnp.where(has_first, owner[col, k1], -1)
    g2 = jnp.where(has_second, owner[col, k2], -1)
    diag = kept[slot, 0] == col
    one = jnp.where(diag, g1, g0)
    two = jnp.where(diag, g2, jnp.maximum(g1, g2))
    return diag, g0, g1, g2, one, two


def kernel(
    kept, owner, x_ref, gain_ref, offset_ref, wq_ref, wk_ref, wv_ref, wg_ref, gb_ref, wb_ref, wo_ref,
    out_ref,
    normed, plane, z_send, z_recv, picked, whole, nb0, nb1, nb2, nb3,
    q_t, gate_t, k_all, v_t, gated, bias_t, wqg_t, wv_t, gb_t, wb_rep,
    s0, s1, p0, p1, m0, m1,
    y_ss, y_rs, c_ss, c_rs, z_ss, z_rs, x_ss, x_rs, n_ss, n_rs,
):
    blk = lax.axis_index("blk")
    rep = lax.axis_index("rep")
    z = blk // PLANE
    y = (blk // 2) % NY
    core = blk % 2
    nbs = (nb0, nb1, nb2, nb3)

    def at_blk(b):
        return {"blk": (b + KEPT) % KEPT}

    def at_y(step):
        return {"blk": z * PLANE + ((y + step + NY) % NY) * 2 + core}

    def at_z(step):
        return {"blk": ((z + step + NZ) % NZ) * PLANE + y * 2 + core}

    def at_x(step):
        return {"rep": (rep + step + NX) % NX}

    mate = {"blk": blk + 1 - 2 * core}

    barrier = pltpu.get_barrier_semaphore()
    greeted = [at_y(s) for s in Y_STEPS] + [at_z(s) for s in Z_STEPS] + [at_x(s) for s in X_STEPS] + [mate]
    greeted += [at_blk(blk - 2 + 3 * core), at_blk(blk - 1 + 3 * core)]
    for device in greeted:
        pl.semaphore_signal(barrier, inc=1, device_id=device, device_id_type=MESH)

    def remote(src, dst, ss, rs, device):
        return pltpu.make_async_remote_copy(
            src_ref=src, dst_ref=dst, send_sem=ss, recv_sem=rs, device_id=device, device_id_type=MESH
        )

    def turned(w):
        return w.astype(F32).T.astype(BF)

    wqg_t[0:W] = turned(wq_ref[...])
    wqg_t[W:] = turned(wg_ref[...])
    wv_t[...] = turned(wv_ref[...])
    gb_t[...] = jnp.broadcast_to(gb_ref[...], (W, W)).T
    wb = wb_ref[...].astype(F32)
    wb_rep[...] = jnp.concatenate([jnp.broadcast_to(wb[:, h : h + 1], (W, ROWS)) for h in range(HEADS)], axis=1)

    lane = lax.broadcasted_iota(I32, (W, W), 1) % ROWS

    def norm_step(t, piece):
        rows, cols = [], []
        for u in range(4):
            i = t * 4 + u
            n = norm_rows(x_ref[i], gain_ref[...], offset_ref[...])
            normed[i] = n
            rows.append(n)
            cols.append(jnp.where(lane == i, wb_rep[...], 0.0).astype(BF))
        return piece + dot(jnp.concatenate(rows, axis=1), jnp.concatenate(cols, axis=0))

    piece = lax.fori_loop(0, ROWS // 4, norm_step, jnp.zeros((W, W), F32))
    plane[core, y] = piece.astype(BF)

    pl.semaphore_wait(barrier, len(greeted))

    y_copies = [
        remote(plane.at[core, y], plane.at[core, y], y_ss.at[n], y_rs.at[n], at_y(s)) for n, s in enumerate(Y_STEPS)
    ]
    for c in y_copies:
        c.start()
    mate_copies = [
        remote(
            normed.at[pl.ds(k * RC, RC)], nbs[k].at[1 + core], n_ss.at[k, 0], n_rs.at[k, 1 + core], mate
        )
        for k in range(CHUNKS)
    ]
    for c in mate_copies:
        c.start()

    def own_step(t, _):
        for u in range(4):
            i = t * 4 + u
            n = normed[i]
            qg = dot_nt(wqg_t[...], n)
            q_t[i] = (qg[:W] * (HD**-0.5 * LOG2E)).astype(BF)
            gate_t[i] = jax.nn.sigmoid(qg[W:] + gb_t[...])
            k_all[i, 0:W] = dot(n, wk_ref[...]).astype(BF)
            v_t[i, :, 0:W] = dot_nt(wv_t[...], n).astype(BF)
        return 0

    lax.fori_loop(0, ROWS // 4, own_step, 0)

    for c in y_copies:
        c.wait_recv()
    cross = remote(plane.at[core], plane.at[core], c_ss, c_rs, mate)
    cross.start()
    side_copies = []
    for k in range(CHUNKS):
        src = normed.at[pl.ds(k * RC, RC)]
        side_copies.append(
            (
                remote(src, nbs[k].at[core], n_ss.at[k, 1], n_rs.at[k, core], at_blk(blk + 2 - core)),
                remote(src, nbs[k].at[2 + core], n_ss.at[k, 2], n_rs.at[k, 2 + core], at_blk(blk - 1 - core)),
            )
        )
        for c in side_copies[-1]:
            c.start()

    remote(plane.at[1 - core], plane.at[1 - core], c_ss, c_rs, mate).wait_recv()

    z_copies = []
    for n, s in enumerate(Z_STEPS):
        there = (z + s + NZ) % NZ
        _, _, _, _, one, two = bias_wants(kept, owner, there * PLANE + y * 2 + core)
        for item, want in enumerate((one, two)):
            local = lax.rem(want + KEPT, PLANE)
            z_send[n, item] = plane[lax.rem(local, 2), local // 2]
        c = remote(z_send.at[n], z_recv.at[z], z_ss.at[n], z_rs.at[n], at_z(s))
        c.start()
        z_copies.append(c)

    diag, g0, g1, g2, one, two = bias_wants(kept, owner, blk)
    for item, want in enumerate((one, two)):
        local = lax.rem(want + KEPT, PLANE)
        z_recv[z, item] = plane[lax.rem(local, 2), local // 2]

    for n, s in enumerate(Z_STEPS):
        remote(z_send.at[n], z_recv.at[(z - s + NZ) % NZ], z_ss.at[n], z_rs.at[n], at_z(s)).wait_recv()

    own = plane[core, y]
    item1 = z_recv[lax.rem(one + KEPT, KEPT) // PLANE, 0]
    item2 = z_recv[lax.rem(two + KEPT, KEPT) // PLANE, 1]
    zero = jnp.zeros_like(own)
    picked[0] = jnp.where(diag, own, item1)
    picked[1] = jnp.where(g1 >= 0, jnp.where(diag, item1, item2), zero)
    picked[2] = jnp.where(g2 >= 0, item2, zero)
    x_copies = [
        remote(picked, whole.at[rep], x_ss.at[n], x_rs.at[n], at_x(s)) for n, s in enumerate(X_STEPS)
    ]
    for c in x_copies:
        c.start()
    whole[rep] = picked[...]

    first, has_first, second, has_second = row_members(kept, blk)
    sel1 = jnp.where(first < 0, 1, 2)
    sel2 = jnp.where(second == -2, 0, jnp.where(second == 1, 2, 3))

    def forward(k):
        remote(normed.at[pl.ds(k * RC, RC)], nbs[k].at[2 * core], n_ss.at[k, 1], n_rs.at[k, 2 * core], mate).wait_recv()
        remote(
            normed.at[pl.ds(k * RC, RC)], nbs[k].at[2 * core + 1], n_ss.at[k, 1], n_rs.at[k, 2 * core + 1], mate
        ).wait_recv()
        c = remote(nbs[k].at[1 + core], nbs[k].at[3 * core], n_ss.at[k, 3], n_rs.at[k, 3 * core], mate)
        c.start()
        return c

    forwards = [forward(0)]

    for n, s in enumerate(X_STEPS):
        remote(picked, whole.at[(rep - s + NX) % NX], x_ss.at[n], x_rs.at[n], at_x(s)).wait_recv()

    group = lax.broadcasted_iota(I32, (W, W), 1) // ROWS
    for t in range(3):
        parts = [whole[r, t].astype(F32) * LOG2E for r in range(NX)]
        if t == 1:
            parts = [jnp.where(has_first, v, MASKED) for v in parts]
        if t == 2:
            parts = [jnp.where(has_second, v, MASKED) for v in parts]
        for h in range(HEADS):
            acc = None
            for r in range(NX):
                shift = ((r - h) * ROWS) % W
                v = pltpu.roll(parts[r], shift, 1) if shift else parts[r]
                acc = v if acc is None else jnp.where(group == r, v, acc)
            bias_t[t * W : (t + 1) * W, h * W : (h + 1) * W] = acc

    row_head = lax.broadcasted_iota(I32, (W, W), 0) // HD

    def score_stage(i, s_ref, m_ref):
        q = q_t[i]
        q_diag = jnp.concatenate(
            [jnp.where(row_head == h, q, jnp.zeros_like(q)) for h in range(HEADS)], axis=1
        )
        s = dot(k_all[i], q_diag) + bias_t[...]
        s_ref[...] = s
        m_ref[...] = jnp.max(s.reshape(48, 8, HEADS * W), axis=0)

    def weight_stage(s_ref, m_ref, p_ref):
        for h in range(HEADS):
            cols = slice(h * W, (h + 1) * W)
            top = jnp.max(m_ref[:, cols], axis=0, keepdims=True)
            p_ref[:, cols] = jnp.exp2(s_ref[:, cols] - top).astype(BF)

    def value_stage(i, p_ref):
        v = v_t[i]
        ones = jnp.ones((16, 3 * W), BF)
        outs = []
        for h in (0, 2):
            r = dot(jnp.concatenate([v[h * HD : (h + 2) * HD], ones], axis=0), p_ref[:, h * W : (h + 2) * W])
            outs.append(r[:HD, :W] * (1.0 / r[2 * HD : 2 * HD + 1, :W]))
            outs.append(r[HD : 2 * HD, W:] * (1.0 / r[2 * HD : 2 * HD + 1, W:]))
        gated[i] = (jnp.concatenate(outs, axis=0) * gate_t[i]).astype(BF)

    ss, ps, ms = (s0, s1), (p0, p1), (m0, m1)

    def step(i, u, score=True, weight=True, value=True):
        if value:
            value_stage(i - 2, ps[u])
        if weight:
            weight_stage(ss[1 - u], ms[1 - u], ps[1 - u])
        if score:
            score_stage(i, ss[u], ms[u])

    def pair_step(t, _):
        step(2 * t, 0)
        step(2 * t + 1, 1)
        return 0

    def out_step(t, _):
        for u in range(4):
            out_ref[t * 4 + u] = dot_tn(gated[t * 4 + u], wo_ref[...]).astype(BF)
        return 0

    for k in range(CHUNKS):
        if k + 1 < CHUNKS:
            forwards.append(forward(k + 1))
        for slot in (2 - core, 3 - 3 * core):
            remote(normed.at[pl.ds(k * RC, RC)], nbs[k].at[slot], n_ss.at[k, 0], n_rs.at[k, slot], mate).wait_recv()

        def key_step(t, _, k=k):
            for u in range(4):
                j = t * 4 + u
                i = k * RC + j
                both = jnp.concatenate([nbs[k][sel1, j], nbs[k][sel2, j]], axis=0)
                k_all[i, W:] = dot(both, wk_ref[...]).astype(BF)
                v_t[i, :, W:] = dot_nt(wv_t[...], both).astype(BF)
            return 0

        lax.fori_loop(0, RC // 4, key_step, 0)
        start = k * RC // 2
        if k == 0:
            step(0, 0, True, False, False)
            step(1, 1, True, True, False)
            start += 1
        lax.fori_loop(start, (k + 1) * RC // 2, pair_step, 0)
        if k:
            lax.fori_loop((k - 1) * RC // 4, k * RC // 4, out_step, 0)
    step(ROWS, 0, False, True, True)
    step(ROWS + 1, 1, False, False, True)
    lax.fori_loop((CHUNKS - 1) * RC // 4, CHUNKS * RC // 4, out_step, 0)

    for c in y_copies + [cross] + z_copies + x_copies + mate_copies + forwards:
        c.wait_send()
    for pair in side_copies:
        for c in pair:
            c.wait_send()


def per_device(
    pair_blocks, kept_pairs, owner, norm_gain, norm_offset, w_query, w_key, w_value, w_gate, gate_bias, w_bias, w_out
):
    vmem = pl.BlockSpec(memory_space=pltpu.VMEM)
    smem = pl.BlockSpec(memory_space=pltpu.SMEM)
    dma = pltpu.SemaphoreType.DMA
    out = pl.pallas_call(
        kernel,
        out_shape=jax.ShapeDtypeStruct((ROWS, W, W), BF),
        in_specs=[smem, smem] + [vmem] * 10,
        out_specs=vmem,
        scratch_shapes=[
            pltpu.VMEM((ROWS, W, W), BF),
            pltpu.VMEM((2, NY, W, W), BF),
            pltpu.VMEM((7, 2, W, W), BF),
            pltpu.VMEM((NZ, 2, W, W), BF),
            pltpu.VMEM((3, W, W), BF),
            pltpu.VMEM((NX, 3, W, W), BF),
        ]
        + [pltpu.VMEM((4, RC, W, W), BF)] * CHUNKS
        + [
            pltpu.VMEM((ROWS, W, W), BF),
            pltpu.VMEM((ROWS, W, W), F32),
            pltpu.VMEM((ROWS, 3 * W, W), BF),
            pltpu.VMEM((ROWS, W, 3 * W), BF),
            pltpu.VMEM((ROWS, W, W), BF),
            pltpu.VMEM((3 * W, HEADS * W), F32),
            pltpu.VMEM((2 * W, W), BF),
            pltpu.VMEM((W, W), BF),
            pltpu.VMEM((W, W), F32),
            pltpu.VMEM((W, W), F32),
        ]
        + [pltpu.VMEM((3 * W, HEADS * W), F32)] * 2
        + [pltpu.VMEM((3 * W, HEADS * W), BF)] * 2
        + [pltpu.VMEM((8, HEADS * W), F32)] * 2
        + [
            dma((7,)), dma((7,)), dma, dma, dma((7,)), dma((7,)), dma((3,)), dma((3,)),
            dma((CHUNKS, 4)), dma((CHUNKS, 4)),
        ],
        compiler_params=pltpu.CompilerParams(
            collective_id=0, has_side_effects=True, vmem_limit_bytes=48 * 2**20
        ),
        name="row_attention",
    )(
        kept_pairs, owner, pair_blocks[0], norm_gain[None], norm_offset[None],
        w_query, w_key, w_value, w_gate, gate_bias[None], w_bias, w_out,
    )
    return out[None]


def solution(mesh):
    return jax.shard_map(
        per_device,
        mesh=mesh,
        in_specs=(P("blk", "rep", None, None),) + (P(),) * 11,
        out_specs=P("blk", "rep", None, None),
        check_vma=False,
    )
```

time: 217 us -> 88.8 us (0.41)
  the two profiles are of different devices: /device:TPU:54 before, /device:TPU:1 now
where the time goes in v1:
time: 88.8 us; the launch traced here: 88.4 us
  Pallas kernels  82.3 us (93%)
  local copies, waits for them, and re-layouts  6.04 us (7%)
    pallas_call x1, Pallas kernels, per_device(): pl.pallas_call(kernel, out_shape=jax.ShapeDtypeStruct((ROWS, W, W), BF),...  82.3 us
    unnamed x27, local copies, waits for them, and re-layouts  6.04 us

profile of v1, /device:TPU:1, one launch (start us, length us, event | category | flops | bytes accessed | tf_op | source)
XLA Modules:
  0.0 88.4 jit_solution(17390784291058276783)
XLA Ops:
  0.0 0.0 copy-start.11
  0.0 0.0 copy-start.10
  0.0 0.7 copy-done.11
  0.7 0.0 copy-start.3
  0.7 0.0 copy-start.9
  0.7 0.1 copy.14.wb_ref
  0.8 0.0 copy-done.10
  0.8 0.0 copy-start.1
  0.8 0.0 copy-start.2
  0.8 0.0 copy-start.7
  0.9 0.0 copy-start.8
  0.9 0.1 copy.13.kept
  1.0 0.5 copy-done.3
  1.4 0.0 copy-done.9
  1.4 0.1 copy-done.1
  1.6 0.0 copy-done.2
  1.6 0.0 copy-done.7
  1.6 0.0 copy-done.8
  1.6 1.2 %copy-done = bf16[1,32,128,128]{3,2,1,0:T(8,128)(2,1)S(1)} copy-done((bf16[1,32,128,128]{3,2,1,0:T(8,128)(2,1)S(1)}, bf16[1,32,128,128]{3,2,1,0:T(8,128)(2,1)}, u32[]{:S(2)}) %copy-start) | copy-done | bytes 1048600
  2.8 0.8 copy-done.4
  3.6 0.8 copy-done.5
  4.4 0.8 copy-done.6
  5.1 82.3 %row_attention.1 = bf16[32,128,128]{2,1,0:T(8,128)(2,1)S(1)} custom-call(s32[128,2]{1,0:T(8,128)S(1)} %copy.13.kept, s32[64,64]{1,0:T(8,128)S(1)} %copy-done.1, bf16[32,128,128]{2,1,0:T(8,128)(2,1)S(1)} %bitcast.6, f32[1,128]{1,0:T(1,128)S(1)} %bitcast.7, f32[1,128]{1,0:T(1,128)S(1)} %bitcast.8, bf16[128,128]{1,0:T(8,128)(2,1)S(1)} %copy-done.2, ...), custom_call_target="tpu_custom_call" | custom-call | tf_op jit(solution)/shard_map/row_attention/pallas_call | solution.py:343
  87.4 1.0 %copy.16 = bf16[1,32,128,128]{3,2,1,0:T(8,128)(2,1)} copy(bf16[1,32,128,128]{3,2,1,0:T(8,128)(2,1)S(1)} %bitcast.5) | data formatting | bytes 2097152
  (4 shorter events, 0.0 us)
Async XLA Ops:
  0.0 0.7 copy-start.11
  0.0 0.8 copy-start.10
  0.7 0.8 copy-start.3
  0.7 0.8 copy-start.9
  0.8 0.8 copy-start.1
  0.8 0.8 copy-start.2
  0.8 0.8 copy-start.7
  0.9 0.8 copy-start.8
  1.6 1.2 %copy-start = (bf16[1,32,128,128]{3,2,1,0:T(8,128)(2,1)S(1)}, bf16[1,32,128,128]{3,2,1,0:T(8,128)(2,1)}, u32[]{:S(2)}) copy-start(bf16[1,32,128,128]{3,2,1,0:T(8,128)(2,1)} %param.12) | copy-start | bytes 3145732
  2.8 0.8 copy-start.4
  3.6 0.8 copy-start.5
  4.4 0.8 copy-start.6

commit v2 on v1

v2 whole, which is shorter than its diff:
```python
import functools

import jax
import jax.numpy as jnp
from jax import lax
from jax.experimental import pallas as pl
from jax.experimental.pallas import tpu as pltpu
from jax.sharding import PartitionSpec as P

F32 = jnp.float32
BF = jnp.bfloat16
I32 = jnp.int32
MESH = pl.DeviceIdType.MESH
LOG2E = 1.4426950408889634
MASKED = -1e30

NZ, NY, NX = 8, 8, 4
PLANE = 2 * NY
KEPT = NZ * PLANE
ROWS = 32
W = 128
HEADS, HD = 4, 32
CHUNKS = 4
PARTS = 2
PH = HEADS // PARTS
KL = W // PARTS
RC = ROWS // CHUNKS
STEPS = (1, -1, 2, -2, 3, -3, 4)
X_STEPS = (1, -1, 2)


def dot(a, b):
    return jnp.dot(a, b, preferred_element_type=F32)


def dot_nt(a, b):
    return lax.dot_general(a, b, (((1,), (1,)), ((), ())), preferred_element_type=F32)


def dot_tn(a, b):
    return lax.dot_general(a, b, (((0,), (0,)), ((), ())), preferred_element_type=F32)


def norm_rows(x, gain, offset):
    v = x.astype(F32)
    d = v - jnp.mean(v, axis=-1, keepdims=True)
    s = jnp.mean(d * d, axis=-1, keepdims=True)
    return (d * lax.rsqrt(s + 1e-05) * gain + offset).astype(BF)


def row_members(kept, slot):
    row = kept[0, slot]

    def same(step):
        other = slot + step
        inside = (other >= 0) & (other < KEPT)
        return inside & (kept[0, jnp.clip(other, 0, KEPT - 1)] == row)

    m1, m2, p1, p2 = same(-1), same(-2), same(1), same(2)
    first = jnp.where(m1, -1, 1)
    second = jnp.where(m1 & p1, 1, jnp.where(m2, -2, 2))
    return first, m1 | p1, second, (m1 & p1) | m2 | p2


def bias_wants(kept, owner, slot):
    first, has_first, second, has_second = row_members(kept, slot)
    col = kept[1, slot]
    k1 = kept[1, jnp.clip(slot + first, 0, KEPT - 1)]
    k2 = kept[1, jnp.clip(slot + second, 0, KEPT - 1)]
    g0 = owner[col, col]
    g1 = jnp.where(has_first, owner[col, k1], -1)
    g2 = jnp.where(has_second, owner[col, k2], -1)
    diag = kept[0, slot] == col
    one = jnp.where(diag, g1, g0)
    two = jnp.where(diag, g2, jnp.maximum(g1, g2))
    return diag, g0, g1, g2, one, two


def kernel(
    x_hbm, kept_hbm, owner_hbm, gain_hbm, offset_hbm, wq_hbm, wk_hbm, wv_hbm, wg_hbm, gb_hbm, wb_hbm, wo_hbm,
    out_ref,
    x_ref, kept, owner, gain_ref, offset_ref, wq_ref, wk_ref, wv_ref, wg_ref, gb_ref, wb_ref, wo_ref,
    normed, plane0, plane1, z_send0, z_send1, z_recv0, z_recv1, picked0, picked1, whole0, whole1,
    nb0, nb1, nb2, nb3,
    q_t, gate_t, k_all, v_t, gated, bias0, bias1, wqg_t, wv_t, gb_t, wb_rep,
    s0, s1, p0, p1, m0, m1,
    in_sem, y_ss, y_rs, c_ss, c_rs, z_ss, z_rs, x_ss, x_rs, n_ss, n_rs,
):
    blk = lax.axis_index("blk")
    rep = lax.axis_index("rep")
    z = blk // PLANE
    y = (blk // 2) % NY
    core = blk % 2
    nbs = (nb0, nb1, nb2, nb3)
    planes, z_sends, z_recvs = (plane0, plane1), (z_send0, z_send1), (z_recv0, z_recv1)
    pickeds, wholes, biases = (picked0, picked1), (whole0, whole1), (bias0, bias1)

    def at_blk(b):
        return {"blk": (b + KEPT) % KEPT}

    def at_y(step):
        return {"blk": z * PLANE + ((y + step + NY) % NY) * 2 + core}

    def at_z(step):
        return {"blk": ((z + step + NZ) % NZ) * PLANE + y * 2 + core}

    def at_x(step):
        return {"rep": (rep + step + NX) % NX}

    mate = {"blk": blk + 1 - 2 * core}

    barrier = pltpu.get_barrier_semaphore()
    greeted = [at_y(s) for s in STEPS] + [at_z(s) for s in STEPS] + [at_x(s) for s in X_STEPS] + [mate]
    greeted += [at_blk(blk - 2 + 3 * core), at_blk(blk - 1 + 3 * core)]
    for device in greeted:
        pl.semaphore_signal(barrier, inc=1, device_id=device, device_id_type=MESH)

    operands = (x_hbm, kept_hbm, owner_hbm, gain_hbm, offset_hbm, wq_hbm, wk_hbm, wv_hbm, wg_hbm, gb_hbm, wb_hbm, wo_hbm)
    places = (x_ref, kept, owner, gain_ref, offset_ref, wq_ref, wk_ref, wv_ref, wg_ref, gb_ref, wb_ref, wo_ref)
    fetches = [pltpu.make_async_copy(o, p, in_sem.at[n]) for n, (o, p) in enumerate(zip(operands, places))]
    for c in fetches:
        c.start()
    for c in fetches:
        c.wait()

    def remote(src, dst, ss, rs, device):
        return pltpu.make_async_remote_copy(
            src_ref=src, dst_ref=dst, send_sem=ss, recv_sem=rs, device_id=device, device_id_type=MESH
        )

    def turned(w):
        return w.astype(F32).T.astype(BF)

    wb = jnp.broadcast_to(wb_ref[...].astype(F32)[:, None], (HEADS, ROWS, W)).reshape(W, W)
    wb_rep[...] = wb.T

    lane = lax.broadcasted_iota(I32, (W, W), 1)

    def norm_step(t, piece):
        rows, cols = [], []
        for u in range(4):
            i = t * 4 + u
            n = norm_rows(x_ref[i], gain_ref[...], offset_ref[...])
            normed[i] = n
            rows.append(n)
            cols.append(jnp.where(lane % ROWS == i, wb_rep[...], 0.0).astype(BF))
        return piece + dot(jnp.concatenate(rows, axis=1), jnp.concatenate(cols, axis=0))

    piece = lax.fori_loop(0, ROWS // 4, norm_step, jnp.zeros((W, W), F32))
    span = PH * ROWS
    place = lax.broadcasted_iota(I32, (KL, W), 1) // span
    for p in range(PARTS):
        packed = None
        for hi in range(PARTS):
            v = piece[hi * KL : (hi + 1) * KL]
            shift = ((hi - p) * span) % W
            v = pltpu.roll(v, shift, 1) if shift else v
            packed = v if packed is None else jnp.where(place == hi, v, packed)
        planes[p][core, (y, z)[p]] = packed.astype(BF)

    gather_at, hand_at = (at_y, at_z), (at_z, at_y)
    gather_pos, hand_pos = (y, z), (z, y)

    def gather_index(p, slot):
        slot = lax.rem(slot + KEPT, KEPT)
        return lax.rem(slot // 2, NY) if p == 0 else slot // PLANE

    def hand_index(p, slot):
        return gather_index(1 - p, slot)

    wants = [
        [bias_wants(kept, owner, ((z + s + NZ) % NZ) * PLANE + y * 2 + core)[4:] for s in STEPS],
        [bias_wants(kept, owner, z * PLANE + ((y + s + NY) % NY) * 2 + core)[4:] for s in STEPS],
    ]
    diag, g0, g1, g2, one, two = bias_wants(kept, owner, blk)
    first, has_first, second, has_second = row_members(kept, blk)
    sel1 = jnp.where(first < 0, 1, 2)
    sel2 = jnp.where(second == -2, 0, jnp.where(second == 1, 2, 3))

    pl.semaphore_wait(barrier, len(greeted))

    y_copies = [
        [
            remote(
                planes[p].at[core, gather_pos[p]], planes[p].at[core, gather_pos[p]],
                y_ss.at[p, n], y_rs.at[p, n], gather_at[p](s),
            )
            for n, s in enumerate(STEPS)
        ]
        for p in range(PARTS)
    ]
    sent = []
    for p in range(PARTS):
        for c in y_copies[p]:
            c.start()
            sent.append(c)

    def send_rows(k):
        src = normed.at[pl.ds(k * RC, RC)]
        for c in (
            remote(src, nbs[k].at[core], n_ss.at[k, 1], n_rs.at[k, core], at_blk(blk + 2 - core)),
            remote(src, nbs[k].at[2 + core], n_ss.at[k, 2], n_rs.at[k, 2 + core], at_blk(blk - 1 - core)),
            remote(src, nbs[k].at[1 + core], n_ss.at[k, 0], n_rs.at[k, 1 + core], mate),
        ):
            c.start()
            sent.append(c)

    def cross(p):
        for c in y_copies[p]:
            c.wait_recv()
        c = remote(planes[p].at[core], planes[p].at[core], c_ss.at[p], c_rs.at[p], mate)
        c.start()
        sent.append(c)

    def spread(p):
        remote(planes[p].at[1 - core], planes[p].at[1 - core], c_ss.at[p], c_rs.at[p], mate).wait_recv()
        for n, s in enumerate(STEPS):
            for item, want in enumerate(wants[p][n]):
                z_sends[p][n, item] = planes[p][lax.rem(want + KEPT, 2), gather_index(p, want)]
            c = remote(z_sends[p].at[n], z_recvs[p].at[hand_pos[p]], z_ss.at[p, n], z_rs.at[p, n], hand_at[p](s))
            c.start()
            sent.append(c)
        for item, want in enumerate((one, two)):
            z_recvs[p][hand_pos[p], item] = planes[p][lax.rem(want + KEPT, 2), gather_index(p, want)]

    def pick(p):
        for n, s in enumerate(STEPS):
            there = (hand_pos[p] - s + NZ) % NZ
            remote(z_sends[p].at[n], z_recvs[p].at[there], z_ss.at[p, n], z_rs.at[p, n], hand_at[p](s)).wait_recv()
        own = planes[p][core, gather_pos[p]]
        item1 = z_recvs[p][hand_index(p, one), 0]
        item2 = z_recvs[p][hand_index(p, two), 1]
        zero = jnp.zeros_like(own)
        pickeds[p][0] = jnp.where(diag, own, item1)
        pickeds[p][1] = jnp.where(g1 >= 0, jnp.where(diag, item1, item2), zero)
        pickeds[p][2] = jnp.where(g2 >= 0, item2, zero)
        for n, s in enumerate(X_STEPS):
            c = remote(pickeds[p], wholes[p].at[rep], x_ss.at[p, n], x_rs.at[p, n], at_x(s))
            c.start()
            sent.append(c)
        wholes[p][rep] = pickeds[p][...]

    group = lax.broadcasted_iota(I32, (KL, W), 1) // ROWS

    def lay_out(p):
        for n, s in enumerate(X_STEPS):
            remote(
                pickeds[p], wholes[p].at[(rep - s + NX) % NX], x_ss.at[p, n], x_rs.at[p, n], at_x(s)
            ).wait_recv()
        for t in range(3):
            parts = [wholes[p][r, t].astype(F32) * LOG2E for r in range(NX)]
            if t == 1:
                parts = [jnp.where(has_first, v, MASKED) for v in parts]
            if t == 2:
                parts = [jnp.where(has_second, v, MASKED) for v in parts]
            for hi in range(PARTS):
                for h in range(PH):
                    acc = None
                    for r in range(NX):
                        shift = ((r - hi * PH - h) * ROWS) % W
                        v = pltpu.roll(parts[r], shift, 1) if shift else parts[r]
                        acc = v if acc is None else jnp.where(group == r, v, acc)
                    biases[p][t * W + hi * KL : t * W + (hi + 1) * KL, h * W : (h + 1) * W] = acc

    def own_step(t, _):
        for u in range(4):
            i = t * 4 + u
            n = normed[i]
            qg = dot_nt(wqg_t[...], n)
            q_t[i] = (qg[:W] * (HD**-0.5 * LOG2E)).astype(BF)
            gate_t[i] = jax.nn.sigmoid(qg[W:] + gb_t[...])
            k_all[i, 0:W] = dot(n, wk_ref[...]).astype(BF)
            v_t[i, :, 0:W] = dot_nt(wv_t[...], n).astype(BF)
        return 0

    def rows_ready(k):
        src = normed.at[pl.ds(k * RC, RC)]
        for slot in (2 * core, 2 * core + 1):
            remote(src, nbs[k].at[slot], n_ss.at[k, 1], n_rs.at[k, slot], mate).wait_recv()
        c = remote(nbs[k].at[1 + core], nbs[k].at[3 * core], n_ss.at[k, 3], n_rs.at[k, 3 * core], mate)
        c.start()
        sent.append(c)

    def rows_used(k):
        src = normed.at[pl.ds(k * RC, RC)]
        for slot in (2 - core, 3 - 3 * core):
            remote(src, nbs[k].at[slot], n_ss.at[k, 0], n_rs.at[k, slot], mate).wait_recv()

        def key_step(t, _):
            for u in range(4):
                j = t * 4 + u
                i = k * RC + j
                both = jnp.concatenate([nbs[k][sel1, j], nbs[k][sel2, j]], axis=0)
                k_all[i, W:] = dot(both, wk_ref[...]).astype(BF)
                v_t[i, :, W:] = dot_nt(wv_t[...], both).astype(BF)
            return 0

        lax.fori_loop(0, RC // 4, key_step, 0)

    row_head = lax.broadcasted_iota(I32, (W, W), 0) // HD

    def score_stage(p, rr, s_ref, m_ref):
        for u in range(2):
            q = q_t[rr * 2 + u]
            q_diag = jnp.concatenate(
                [jnp.where(row_head == h, q, jnp.zeros_like(q)) for h in range(p * PH, (p + 1) * PH)], axis=1
            )
            s = dot(k_all[rr * 2 + u], q_diag) + biases[p][...]
            s_ref[u] = s
            m_ref[u] = jnp.max(s.reshape(48, 8, PH * W), axis=0)

    def weight_stage(s_ref, m_ref, p_ref):
        for u in range(2):
            for h in range(PH):
                cols = slice(h * W, (h + 1) * W)
                top = jnp.max(m_ref[u, :, cols], axis=0, keepdims=True)
                p_ref[u, :, cols] = jnp.exp2(s_ref[u, :, cols] - top).astype(BF)

    def value_stage(p, rr, p_ref):
        heads = slice(p * PH * HD, (p + 1) * PH * HD)
        ones = jnp.ones((16, 3 * W), BF)
        for u in range(2):
            i = rr * 2 + u
            r = dot(jnp.concatenate([v_t[i, heads], ones], axis=0), p_ref[u])
            outs = []
            for h in range(PH):
                cols = slice(h * W, (h + 1) * W)
                outs.append(r[h * HD : (h + 1) * HD, cols] * (1.0 / r[PH * HD : PH * HD + 1, cols]))
            gated[i, heads] = (jnp.concatenate(outs, axis=0) * gate_t[i, heads]).astype(BF)

    def step(rr, before=True, here=True):
        if before:
            value_stage(0, rr - 1, p0)
            weight_stage(s1, m1, p1)
        if here:
            score_stage(0, rr, s0, m0)
        if before:
            value_stage(1, rr - 1, p1)
        if here:
            weight_stage(s0, m0, p0)
            score_stage(1, rr, s1, m1)

    def attend(lo, hi):
        def row_step(rr, _):
            step(rr)
            return 0

        if lo == 0:
            step(0, before=False)
        lax.fori_loop(max(lo, 1), hi, row_step, 0)
        if hi == ROWS // 2:
            step(hi, here=False)

    send_rows(0)
    wqg_t[0:W] = turned(wq_ref[...])
    wqg_t[W:] = turned(wg_ref[...])
    cross(0)
    cross(1)
    send_rows(1)
    spread(0)
    spread(1)
    send_rows(2)
    wv_t[...] = turned(wv_ref[...])
    gb_t[...] = jnp.broadcast_to(gb_ref[...], (W, W)).T
    lax.fori_loop(0, ROWS // 4, own_step, 0)
    pick(0)
    pick(1)
    send_rows(3)
    rows_ready(0)
    rows_used(0)
    rows_ready(1)
    lay_out(0)
    lay_out(1)
    for k in range(CHUNKS):
        if k:
            rows_used(k)
        if k and k + 1 < CHUNKS:
            rows_ready(k + 1)
        attend(k * RC // 2, (k + 1) * RC // 2)

    def out_step(t, _):
        for u in range(8):
            out_ref[t * 8 + u] = dot_tn(gated[t * 8 + u], wo_ref[...]).astype(BF)
        return 0

    lax.fori_loop(0, ROWS // 8, out_step, 0)

    for c in sent:
        c.wait_send()


def per_device(
    pair_blocks, kept_pairs, owner, norm_gain, norm_offset, w_query, w_key, w_value, w_gate, gate_bias, w_bias, w_out
):
    hbm = pl.BlockSpec(memory_space=pltpu.HBM)
    dma = pltpu.SemaphoreType.DMA
    operands = (
        pair_blocks[0], kept_pairs.T, owner, norm_gain[None], norm_offset[None],
        w_query, w_key, w_value, w_gate, gate_bias[None], w_bias.T, w_out,
    )
    out = pl.pallas_call(
        kernel,
        out_shape=jax.ShapeDtypeStruct((ROWS, W, W), BF),
        in_specs=[hbm] * len(operands),
        out_specs=pl.BlockSpec(memory_space=pltpu.VMEM),
        scratch_shapes=[
            (pltpu.SMEM if o.dtype == I32 else pltpu.VMEM)(o.shape, o.dtype) for o in operands
        ]
        + [pltpu.VMEM((ROWS, W, W), BF)]
        + [pltpu.VMEM((2, NY, KL, W), BF)] * PARTS
        + [pltpu.VMEM((7, 2, KL, W), BF)] * PARTS
        + [pltpu.VMEM((NZ, 2, KL, W), BF)] * PARTS
        + [pltpu.VMEM((3, KL, W), BF)] * PARTS
        + [pltpu.VMEM((NX, 3, KL, W), BF)] * PARTS
        + [pltpu.VMEM((4, RC, W, W), BF)] * CHUNKS
        + [
            pltpu.VMEM((ROWS, W, W), BF),
            pltpu.VMEM((ROWS, W, W), F32),
            pltpu.VMEM((ROWS, 3 * W, W), BF),
            pltpu.VMEM((ROWS, W, 3 * W), BF),
            pltpu.VMEM((ROWS, W, W), BF),
        ]
        + [pltpu.VMEM((3 * W, PH * W), F32)] * PARTS
        + [
            pltpu.VMEM((2 * W, W), BF),
            pltpu.VMEM((W, W), BF),
            pltpu.VMEM((W, W), F32),
            pltpu.VMEM((W, W), F32),
        ]
        + [pltpu.VMEM((2, 3 * W, PH * W), F32)] * 2
        + [pltpu.VMEM((2, 3 * W, PH * W), BF)] * 2
        + [pltpu.VMEM((2, 8, PH * W), F32)] * 2
        + [
            dma((len(operands),)),
            dma((PARTS, 7)), dma((PARTS, 7)), dma((PARTS,)), dma((PARTS,)), dma((PARTS, 7)), dma((PARTS, 7)),
            dma((PARTS, 3)), dma((PARTS, 3)), dma((CHUNKS, 4)), dma((CHUNKS, 4)),
        ],
        compiler_params=pltpu.CompilerParams(
            collective_id=0, has_side_effects=True, vmem_limit_bytes=40 * 2**20
        ),
        name="row_attention",
    )(*operands)
    return out[None]


def solution(mesh):
    return jax.shard_map(
        per_device,
        mesh=mesh,
        in_specs=(P("blk", "rep", None, None),) + (P(),) * 11,
        out_specs=P("blk", "rep", None, None),
        check_vma=False,
    )
```

time: 88.8 us -> 68.2 us (0.77)
  Pallas kernels: 82.3 us -> 60.2 us
  local copies, waits for them, and re-layouts: 6.04 us -> 7.45 us
    pallas_call x1, Pallas kernels: 82.3 us -> 60.2 us  [per_device(): pl.pallas_call(kernel, out_shape=jax.ShapeDtypeStruct((ROWS, W, W), BF),...]
    unnamed x27 -> x25, local copies, waits for them, and re-layouts: 6.04 us -> 7.45 us
where the time goes in v2:
time: 68.2 us; the launch traced here: 67.7 us
  Pallas kernels  60.2 us (88%)
  local copies, waits for them, and re-layouts  7.45 us (11%)
    pallas_call x1, Pallas kernels, per_device(): pl.pallas_call(kernel, out_shape=jax.ShapeDtypeStruct((ROWS, W, W), BF),...  60.2 us
    unnamed x25, local copies, waits for them, and re-layouts  7.45 us

profile of v2, /device:TPU:1, one launch (start us, length us, event | category | flops | bytes accessed | tf_op | source)
XLA Modules:
  0.0 67.7 jit_solution(91405636998161737)
XLA Ops:
  0.0 0.0 copy-start.8
  0.0 0.0 copy-start.10
  0.0 0.0 copy-start.11
  0.0 0.0 copy-start.7
  0.0 0.0 copy-start.9
  0.0 0.7 copy-done.8
  0.7 0.0 copy-done.10
  0.7 0.0 copy-done.11
  0.7 0.0 copy-done.7
  0.7 0.0 copy-done.9
  0.7 0.0 copy-start
  0.7 1.2 %copy-done = bf16[1,32,128,128]{3,2,1,0:T(8,128)(2,1)S(1)} copy-done((bf16[1,32,128,128]{3,2,1,0:T(8,128)(2,1)S(1)}, bf16[1,32,128,128]{3,2,1,0:T(8,128)(2,1)}, u32[]{:S(2)}) %copy-start) | copy-done | bytes 1048600
  2.0 0.0 copy-start.1
  2.0 0.8 %copy-done.1 = s32[64,64]{1,0:T(8,128)S(1)} copy-done((s32[64,64]{1,0:T(8,128)S(1)}, s32[64,64]{1,0:T(8,128)}, u32[]{:S(2)}) %copy-start.1) | copy-done | bytes 16408
  2.7 0.0 copy-start.2
  2.7 0.8 %copy-done.2 = bf16[128,128]{1,0:T(8,128)(2,1)S(1)} copy-done((bf16[128,128]{1,0:T(8,128)(2,1)S(1)}, bf16[128,128]{1,0:T(8,128)(2,1)}, u32[]{:S(2)}) %copy-start.2) | copy-done | bytes 32792
  3.5 0.0 copy-start.3
  3.5 0.8 %copy-done.3 = bf16[128,128]{1,0:T(8,128)(2,1)S(1)} copy-done((bf16[128,128]{1,0:T(8,128)(2,1)S(1)}, bf16[128,128]{1,0:T(8,128)(2,1)}, u32[]{:S(2)}) %copy-start.3) | copy-done | bytes 32792
  4.2 0.0 copy-start.4
  4.2 0.8 %copy-done.4 = bf16[128,128]{1,0:T(8,128)(2,1)S(1)} copy-done((bf16[128,128]{1,0:T(8,128)(2,1)S(1)}, bf16[128,128]{1,0:T(8,128)(2,1)}, u32[]{:S(2)}) %copy-start.4) | copy-done | bytes 32792
  5.0 0.8 %copy-done.5 = bf16[128,128]{1,0:T(8,128)(2,1)S(1)} copy-done((bf16[128,128]{1,0:T(8,128)(2,1)S(1)}, bf16[128,128]{1,0:T(8,128)(2,1)}, u32[]{:S(2)}) %copy-start.5) | copy-done | bytes 32792
  5.8 0.8 %copy-done.6 = bf16[128,128]{1,0:T(8,128)(2,1)S(1)} copy-done((bf16[128,128]{1,0:T(8,128)(2,1)S(1)}, bf16[128,128]{1,0:T(8,128)(2,1)}, u32[]{:S(2)}) %copy-start.6) | copy-done | bytes 32792
  6.5 60.2 %row_attention.1 = bf16[32,128,128]{2,1,0:T(8,128)(2,1)S(1)} custom-call(bf16[32,128,128]{2,1,0:T(8,128)(2,1)S(1)} %bitcast.8, s32[2,128]{1,0:T(2,128)S(1)} %bitcast.9, s32[64,64]{1,0:T(8,128)S(1)} %copy-done.1, f32[1,128]{1,0:T(1,128)S(1)} %bitcast.11, f32[1,128]{1,0:T(1,128)S(1)} %bitcast.12, bf16[128,128]{1,0:T(8,128)(2,1)S(1)} %copy-done.2, ...), custom_call_target="tpu_custom_call" | custom-call | tf_op jit(solution)/shard_map/row_attention/pallas_call | solution.py:401
  66.7 1.0 %copy.14 = bf16[1,32,128,128]{3,2,1,0:T(8,128)(2,1)} copy(bf16[1,32,128,128]{3,2,1,0:T(8,128)(2,1)S(1)} %bitcast.7) | data formatting | bytes 2097152
  (2 shorter events, 0.0 us)
Async XLA Ops:
  0.0 0.7 %copy-start.8 = (bf16[128,4]{0,1:T(4,128)(2,1)S(1)}, bf16[128,4]{0,1:T(4,128)(2,1)}, u32[]{:S(2)}) copy-start(bf16[128,4]{0,1:T(4,128)(2,1)} %param.22) | copy-start | bytes 3076
  0.0 0.7 %copy-start.10 = (f32[128]{0:T(128)S(1)}, f32[128]{0:T(128)}, u32[]{:S(2)}) copy-start(f32[128]{0:T(128)} %param.16) | copy-start | bytes 1540
  0.0 0.7 %copy-start.11 = (f32[128]{0:T(128)S(1)}, f32[128]{0:T(128)}, u32[]{:S(2)}) copy-start(f32[128]{0:T(128)} %param.21) | copy-start | bytes 1540
  0.0 0.7 %copy-start.7 = (s32[128,2]{0,1:T(2,128)S(1)}, s32[128,2]{0,1:T(2,128)}, u32[]{:S(2)}) copy-start(s32[128,2]{0,1:T(2,128)} %param.13) | copy-start | bytes 3076
  0.0 0.7 %copy-start.9 = (f32[128]{0:T(128)S(1)}, f32[128]{0:T(128)}, u32[]{:S(2)}) copy-start(f32[128]{0:T(128)} %param.15) | copy-start | bytes 1540
  0.7 1.2 %copy-start = (bf16[1,32,128,128]{3,2,1,0:T(8,128)(2,1)S(1)}, bf16[1,32,128,128]{3,2,1,0:T(8,128)(2,1)}, u32[]{:S(2)}) copy-start(bf16[1,32,128,128]{3,2,1,0:T(8,128)(2,1)} %param.12) | copy-start | bytes 3145732
  2.0 0.8 %copy-start.1 = (s32[64,64]{1,0:T(8,128)S(1)}, s32[64,64]{1,0:T(8,128)}, u32[]{:S(2)}) copy-start(s32[64,64]{1,0:T(8,128)} %owner_hbm.1) | copy-start | bytes 49156
  2.7 0.8 %copy-start.2 = (bf16[128,128]{1,0:T(8,128)(2,1)S(1)}, bf16[128,128]{1,0:T(8,128)(2,1)}, u32[]{:S(2)}) copy-start(bf16[128,128]{1,0:T(8,128)(2,1)} %wq_hbm.1) | copy-start | bytes 98308
  3.5 0.8 %copy-start.3 = (bf16[128,128]{1,0:T(8,128)(2,1)S(1)}, bf16[128,128]{1,0:T(8,128)(2,1)}, u32[]{:S(2)}) copy-start(bf16[128,128]{1,0:T(8,128)(2,1)} %wk_hbm.1) | copy-start | bytes 98308
  4.2 0.8 %copy-start.4 = (bf16[128,128]{1,0:T(8,128)(2,1)S(1)}, bf16[128,128]{1,0:T(8,128)(2,1)}, u32[]{:S(2)}) copy-start(bf16[128,128]{1,0:T(8,128)(2,1)} %wv_hbm.1) | copy-start | bytes 98308
  5.0 0.8 %copy-start.5 = (bf16[128,128]{1,0:T(8,128)(2,1)S(1)}, bf16[128,128]{1,0:T(8,128)(2,1)}, u32[]{:S(2)}) copy-start(bf16[128,128]{1,0:T(8,128)(2,1)} %wg_hbm.1) | copy-start | bytes 98308
  5.7 0.8 %copy-start.6 = (bf16[128,128]{1,0:T(8,128)(2,1)S(1)}, bf16[128,128]{1,0:T(8,128)(2,1)}, u32[]{:S(2)}) copy-start(bf16[128,128]{1,0:T(8,128)(2,1)} %wo_hbm.1) | copy-start | bytes 98308

commit v3 on v2

--- a/solution.py
+++ b/solution.py
@@ -25,8 +25,8 @@
 PH = HEADS // PARTS
 KL = W // PARTS
 RC = ROWS // CHUNKS
-STEPS = (1, -1, 2, -2, 3, -3, 4)
-X_STEPS = (1, -1, 2)
+STEPS = (4, 3, -3, 2, -2, 1, -1)
+X_STEPS = (2, 1, -1)
 
 
 def dot(a, b):
@@ -111,7 +111,7 @@
 
     barrier = pltpu.get_barrier_semaphore()
     greeted = [at_y(s) for s in STEPS] + [at_z(s) for s in STEPS] + [at_x(s) for s in X_STEPS] + [mate]
-    greeted += [at_blk(blk - 2 + 3 * core), at_blk(blk - 1 + 3 * core)]
+    greeted += [at_blk(blk - 2), at_blk(blk + 2)]
     for device in greeted:
         pl.semaphore_signal(barrier, inc=1, device_id=device, device_id_type=MESH)
 
@@ -120,8 +120,8 @@
     fetches = [pltpu.make_async_copy(o, p, in_sem.at[n]) for n, (o, p) in enumerate(zip(operands, places))]
     for c in fetches:
         c.start()
-    for c in fetches:
-        c.wait()
+    for n in (0, 3, 4, 10):
+        fetches[n].wait()
 
     def remote(src, dst, ss, rs, device):
         return pltpu.make_async_remote_copy(
@@ -145,6 +145,18 @@
             rows.append(n)
             cols.append(jnp.where(lane % ROWS == i, wb_rep[...], 0.0).astype(BF))
         return piece + dot(jnp.concatenate(rows, axis=1), jnp.concatenate(cols, axis=0))
+
+    sent = []
+
+    def send_rows(k):
+        src = normed.at[pl.ds(k * RC, RC)]
+        for c in (
+            remote(src, nbs[k].at[0], n_ss.at[k, 1], n_rs.at[k, 0], at_blk(blk + 2)),
+            remote(src, nbs[k].at[3], n_ss.at[k, 2], n_rs.at[k, 3], at_blk(blk - 2)),
+            remote(src, nbs[k].at[1 + core], n_ss.at[k, 0], n_rs.at[k, 1 + core], mate),
+        ):
+            c.start()
+            sent.append(c)
 
     piece = lax.fori_loop(0, ROWS // 4, norm_step, jnp.zeros((W, W), F32))
     span = PH * ROWS
@@ -168,15 +180,6 @@
     def hand_index(p, slot):
         return gather_index(1 - p, slot)
 
-    wants = [
-        [bias_wants(kept, owner, ((z + s + NZ) % NZ) * PLANE + y * 2 + core)[4:] for s in STEPS],
-        [bias_wants(kept, owner, z * PLANE + ((y + s + NY) % NY) * 2 + core)[4:] for s in STEPS],
-    ]
-    diag, g0, g1, g2, one, two = bias_wants(kept, owner, blk)
-    first, has_first, second, has_second = row_members(kept, blk)
-    sel1 = jnp.where(first < 0, 1, 2)
-    sel2 = jnp.where(second == -2, 0, jnp.where(second == 1, 2, 3))
-
     pl.semaphore_wait(barrier, len(greeted))
 
     y_copies = [
@@ -189,21 +192,21 @@
         ]
         for p in range(PARTS)
     ]
-    sent = []
     for p in range(PARTS):
         for c in y_copies[p]:
             c.start()
             sent.append(c)
 
-    def send_rows(k):
-        src = normed.at[pl.ds(k * RC, RC)]
-        for c in (
-            remote(src, nbs[k].at[core], n_ss.at[k, 1], n_rs.at[k, core], at_blk(blk + 2 - core)),
-            remote(src, nbs[k].at[2 + core], n_ss.at[k, 2], n_rs.at[k, 2 + core], at_blk(blk - 1 - core)),
-            remote(src, nbs[k].at[1 + core], n_ss.at[k, 0], n_rs.at[k, 1 + core], mate),
-        ):
-            c.start()
-            sent.append(c)
+    for n in (1, 2, 5, 6, 7, 8, 9, 11):
+        fetches[n].wait()
+    wants = [
+        [bias_wants(kept, owner, ((z + s + NZ) % NZ) * PLANE + y * 2 + core)[4:] for s in STEPS],
+        [bias_wants(kept, owner, z * PLANE + ((y + s + NY) % NY) * 2 + core)[4:] for s in STEPS],
+    ]
+    diag, g0, g1, g2, one, two = bias_wants(kept, owner, blk)
+    first, has_first, second, has_second = row_members(kept, blk)
+    sel1 = jnp.where(first < 0, 1, 2)
+    sel2 = jnp.where(second == -2, 0, jnp.where(second == 1, 2, 3))
 
     def cross(p):
         for c in y_copies[p]:
@@ -275,15 +278,15 @@
 
     def rows_ready(k):
         src = normed.at[pl.ds(k * RC, RC)]
-        for slot in (2 * core, 2 * core + 1):
+        for slot in (0, 3):
             remote(src, nbs[k].at[slot], n_ss.at[k, 1], n_rs.at[k, slot], mate).wait_recv()
-        c = remote(nbs[k].at[1 + core], nbs[k].at[3 * core], n_ss.at[k, 3], n_rs.at[k, 3 * core], mate)
+        c = remote(nbs[k].at[3 - 3 * core], nbs[k].at[2 - core], n_ss.at[k, 3], n_rs.at[k, 2 - core], mate)
         c.start()
         sent.append(c)
 
     def rows_used(k):
         src = normed.at[pl.ds(k * RC, RC)]
-        for slot in (2 - core, 3 - 3 * core):
+        for slot in (2 - core, 1 + core):
             remote(src, nbs[k].at[slot], n_ss.at[k, 0], n_rs.at[k, slot], mate).wait_recv()
 
         def key_step(t, _):
@@ -351,21 +354,26 @@
         if hi == ROWS // 2:
             step(hi, here=False)
 
-    send_rows(0)
+    def out_step(t, _):
+        for u in range(RC):
+            out_ref[t * RC + u] = dot_tn(gated[t * RC + u], wo_ref[...]).astype(BF)
+        return 0
+
     wqg_t[0:W] = turned(wq_ref[...])
     wqg_t[W:] = turned(wg_ref[...])
     cross(0)
     cross(1)
-    send_rows(1)
+    send_rows(0)
     spread(0)
     spread(1)
-    send_rows(2)
+    send_rows(1)
     wv_t[...] = turned(wv_ref[...])
     gb_t[...] = jnp.broadcast_to(gb_ref[...], (W, W)).T
     lax.fori_loop(0, ROWS // 4, own_step, 0)
+    send_rows(2)
+    send_rows(3)
     pick(0)
     pick(1)
-    send_rows(3)
     rows_ready(0)
     rows_used(0)
     rows_ready(1)
@@ -377,13 +385,9 @@
         if k and k + 1 < CHUNKS:
             rows_ready(k + 1)
         attend(k * RC // 2, (k + 1) * RC // 2)
-
-    def out_step(t, _):
-        for u in range(8):
-            out_ref[t * 8 + u] = dot_tn(gated[t * 8 + u], wo_ref[...]).astype(BF)
-        return 0
-
-    lax.fori_loop(0, ROWS // 8, out_step, 0)
+        if k:
+            lax.fori_loop(k - 1, k, out_step, 0)
+    lax.fori_loop(CHUNKS - 1, CHUNKS, out_step, 0)
 
     for c in sent:
         c.wait_send()
@@ -436,7 +440,7 @@
             dma((PARTS, 3)), dma((PARTS, 3)), dma((CHUNKS, 4)), dma((CHUNKS, 4)),
         ],
         compiler_params=pltpu.CompilerParams(
-            collective_id=0, has_side_effects=True, vmem_limit_bytes=40 * 2**20
+            collective_id=0, has_side_effects=True, vmem_limit_bytes=60 * 2**20
         ),
         name="row_attention",
     )(*operands)

time: 68.2 us -> 61 us (0.89)
  local copies, waits for them, and re-layouts: 7.45 us -> 2.31 us
  Pallas kernels: 60.2 us -> 58.5 us
    unnamed x25 -> x1, local copies, waits for them, and re-layouts: 7.45 us -> 2.31 us
    pallas_call x1, Pallas kernels: 60.2 us -> 58.5 us  [per_device(): pl.pallas_call(kernel, out_shape=jax.ShapeDtypeStruct((ROWS, W, W), BF),...]
where the time goes in v3:
time: 61 us; the launch traced here: 60.9 us
  Pallas kernels  58.5 us (96%)
  local copies, waits for them, and re-layouts  2.31 us (4%)
    pallas_call x1, Pallas kernels, per_device(): pl.pallas_call(kernel, out_shape=jax.ShapeDtypeStruct((ROWS, W, W), BF),...  58.5 us
    unnamed x1, local copies, waits for them, and re-layouts  2.31 us

profile of v3, /device:TPU:1, one launch (start us, length us, event | category | flops | bytes accessed | tf_op | source)
XLA Modules:
  0.0 60.9 jit_solution(4883102069862576735)
XLA Ops:
  0.0 58.5 %row_attention.1 = bf16[32,128,128]{2,1,0:T(8,128)(2,1)} custom-call(bf16[32,128,128]{2,1,0:T(8,128)(2,1)} %bitcast.8, s32[2,128]{1,0:T(2,128)} %bitcast.9, s32[64,64]{1,0:T(8,128)} %owner_hbm.1, f32[1,128]{1,0:T(1,128)} %bitcast.11, f32[1,128]{1,0:T(1,128)} %bitcast.12, bf16[128,128]{1,0:T(8,128)(2,1)} %wq_hbm.1, bf16[128,128]{1,0:T(8,128)(2,1)} %wk_hbm.1, ...), custom_call_target="tpu_custom_call" | custom-call | tf_op jit(solution)/shard_map/row_attention/pallas_call | solution.py:405
  58.6 2.3 %copy.14 = bf16[1,32,128,128]{3,2,1,0:T(8,128)(2,1)} copy(bf16[1,32,128,128]{3,2,1,0:T(8,128)(2,1)} %bitcast.7) | data formatting | bytes 2097152

commit v4 on v3

--- a/solution.py
+++ b/solution.py
@@ -20,7 +20,7 @@
 ROWS = 32
 W = 128
 HEADS, HD = 4, 32
-CHUNKS = 4
+CHUNKS = 8
 PARTS = 2
 PH = HEADS // PARTS
 KL = W // PARTS
@@ -78,20 +78,18 @@
 
 def kernel(
     x_hbm, kept_hbm, owner_hbm, gain_hbm, offset_hbm, wq_hbm, wk_hbm, wv_hbm, wg_hbm, gb_hbm, wb_hbm, wo_hbm,
-    out_ref,
+    out_hbm,
     x_ref, kept, owner, gain_ref, offset_ref, wq_ref, wk_ref, wv_ref, wg_ref, gb_ref, wb_ref, wo_ref,
     normed, plane0, plane1, z_send0, z_send1, z_recv0, z_recv1, picked0, picked1, whole0, whole1,
-    nb0, nb1, nb2, nb3,
-    q_t, gate_t, k_all, v_t, gated, bias0, bias1, wqg_t, wv_t, gb_t, wb_rep,
+    own_piece, whole_own, q_t, gate_t, k_all, v_t, gated, out_ref, bias0, bias1, wqg_t, wv_t, gb_t, wb_rep,
     s0, s1, p0, p1, m0, m1,
-    in_sem, y_ss, y_rs, c_ss, c_rs, z_ss, z_rs, x_ss, x_rs, n_ss, n_rs,
+    in_sem, out_sem, y_ss, y_rs, c_ss, c_rs, z_ss, z_rs, o_ss, o_rs, x_ss, x_rs, n_ss, n_rs, *nbs
 ):
     blk = lax.axis_index("blk")
     rep = lax.axis_index("rep")
     z = blk // PLANE
     y = (blk // 2) % NY
     core = blk % 2
-    nbs = (nb0, nb1, nb2, nb3)
     planes, z_sends, z_recvs = (plane0, plane1), (z_send0, z_send1), (z_recv0, z_recv1)
     pickeds, wholes, biases = (picked0, picked1), (whole0, whole1), (bias0, bias1)
 
@@ -168,6 +166,7 @@
             shift = ((hi - p) * span) % W
             v = pltpu.roll(v, shift, 1) if shift else v
             packed = v if packed is None else jnp.where(place == hi, v, packed)
+        own_piece[p] = packed.astype(BF)
         planes[p][core, (y, z)[p]] = packed.astype(BF)
 
     gather_at, hand_at = (at_y, at_z), (at_z, at_y)
@@ -196,6 +195,11 @@
         for c in y_copies[p]:
             c.start()
             sent.append(c)
+    for n, s in enumerate(X_STEPS):
+        c = remote(own_piece, whole_own.at[rep], o_ss.at[n], o_rs.at[n], at_x(s))
+        c.start()
+        sent.append(c)
+    whole_own[rep] = own_piece[...]
 
     for n in (1, 2, 5, 6, 7, 8, 9, 11):
         fetches[n].wait()
@@ -230,13 +234,8 @@
         for n, s in enumerate(STEPS):
             there = (hand_pos[p] - s + NZ) % NZ
             remote(z_sends[p].at[n], z_recvs[p].at[there], z_ss.at[p, n], z_rs.at[p, n], hand_at[p](s)).wait_recv()
-        own = planes[p][core, gather_pos[p]]
-        item1 = z_recvs[p][hand_index(p, one), 0]
-        item2 = z_recvs[p][hand_index(p, two), 1]
-        zero = jnp.zeros_like(own)
-        pickeds[p][0] = jnp.where(diag, own, item1)
-        pickeds[p][1] = jnp.where(g1 >= 0, jnp.where(diag, item1, item2), zero)
-        pickeds[p][2] = jnp.where(g2 >= 0, item2, zero)
+        pickeds[p][0] = z_recvs[p][hand_index(p, one), 0]
+        pickeds[p][1] = z_recvs[p][hand_index(p, two), 1]
         for n, s in enumerate(X_STEPS):
             c = remote(pickeds[p], wholes[p].at[rep], x_ss.at[p, n], x_rs.at[p, n], at_x(s))
             c.start()
@@ -246,16 +245,25 @@
     group = lax.broadcasted_iota(I32, (KL, W), 1) // ROWS
 
     def lay_out(p):
+        if p == 0:
+            for n, s in enumerate(X_STEPS):
+                remote(own_piece, whole_own.at[(rep - s + NX) % NX], o_ss.at[n], o_rs.at[n], at_x(s)).wait_recv()
         for n, s in enumerate(X_STEPS):
             remote(
                 pickeds[p], wholes[p].at[(rep - s + NX) % NX], x_ss.at[p, n], x_rs.at[p, n], at_x(s)
             ).wait_recv()
+        owns = [whole_own[r, p].astype(F32) * LOG2E for r in range(NX)]
+        ones = [wholes[p][r, 0].astype(F32) * LOG2E for r in range(NX)]
+        twos = [wholes[p][r, 1].astype(F32) * LOG2E for r in range(NX)]
         for t in range(3):
-            parts = [wholes[p][r, t].astype(F32) * LOG2E for r in range(NX)]
+            if t == 0:
+                parts = [jnp.where(diag, a, b) for a, b in zip(owns, ones)]
             if t == 1:
-                parts = [jnp.where(has_first, v, MASKED) for v in parts]
+                blank = jnp.where(has_first, 0.0, MASKED)
+                parts = [jnp.where(g1 >= 0, jnp.where(diag, a, b), blank) for a, b in zip(ones, twos)]
             if t == 2:
-                parts = [jnp.where(has_second, v, MASKED) for v in parts]
+                blank = jnp.where(has_second, 0.0, MASKED)
+                parts = [jnp.where(g2 >= 0, b, blank) for b in twos]
             for hi in range(PARTS):
                 for h in range(PH):
                     acc = None
@@ -354,31 +362,37 @@
         if hi == ROWS // 2:
             step(hi, here=False)
 
-    def out_step(t, _):
-        for u in range(RC):
-            out_ref[t * RC + u] = dot_tn(gated[t * RC + u], wo_ref[...]).astype(BF)
-        return 0
+    def write(k):
+        for i in range(k * RC, (k + 1) * RC):
+            out_ref[i] = dot_tn(gated[i], wo_ref[...]).astype(BF)
+        rows = pl.ds(k * RC, RC)
+        c = pltpu.make_async_copy(out_ref.at[rows], out_hbm.at[rows], out_sem.at[k])
+        c.start()
+        return c
 
     wqg_t[0:W] = turned(wq_ref[...])
     wqg_t[W:] = turned(wg_ref[...])
     cross(0)
     cross(1)
     send_rows(0)
+    send_rows(1)
     spread(0)
     spread(1)
-    send_rows(1)
+    send_rows(2)
+    send_rows(3)
     wv_t[...] = turned(wv_ref[...])
     gb_t[...] = jnp.broadcast_to(gb_ref[...], (W, W)).T
     lax.fori_loop(0, ROWS // 4, own_step, 0)
-    send_rows(2)
-    send_rows(3)
+    for k in range(4, CHUNKS):
+        send_rows(k)
     pick(0)
     pick(1)
     rows_ready(0)
+    rows_ready(1)
     rows_used(0)
-    rows_ready(1)
     lay_out(0)
     lay_out(1)
+    writes = []
     for k in range(CHUNKS):
         if k:
             rows_used(k)
@@ -386,9 +400,11 @@
             rows_ready(k + 1)
         attend(k * RC // 2, (k + 1) * RC // 2)
         if k:
-            lax.fori_loop(k - 1, k, out_step, 0)
-    lax.fori_loop(CHUNKS - 1, CHUNKS, out_step, 0)
-
+            writes.append(write(k - 1))
+    writes.append(write(CHUNKS - 1))
+
+    for c in writes:
+        c.wait()
     for c in sent:
         c.wait_send()
 
@@ -406,7 +422,7 @@
         kernel,
         out_shape=jax.ShapeDtypeStruct((ROWS, W, W), BF),
         in_specs=[hbm] * len(operands),
-        out_specs=pl.BlockSpec(memory_space=pltpu.VMEM),
+        out_specs=hbm,
         scratch_shapes=[
             (pltpu.SMEM if o.dtype == I32 else pltpu.VMEM)(o.shape, o.dtype) for o in operands
         ]
@@ -414,14 +430,16 @@
         + [pltpu.VMEM((2, NY, KL, W), BF)] * PARTS
         + [pltpu.VMEM((7, 2, KL, W), BF)] * PARTS
         + [pltpu.VMEM((NZ, 2, KL, W), BF)] * PARTS
-        + [pltpu.VMEM((3, KL, W), BF)] * PARTS
-        + [pltpu.VMEM((NX, 3, KL, W), BF)] * PARTS
-        + [pltpu.VMEM((4, RC, W, W), BF)] * CHUNKS
+        + [pltpu.VMEM((2, KL, W), BF)] * PARTS
+        + [pltpu.VMEM((NX, 2, KL, W), BF)] * PARTS
         + [
+            pltpu.VMEM((PARTS, KL, W), BF),
+            pltpu.VMEM((NX, PARTS, KL, W), BF),
             pltpu.VMEM((ROWS, W, W), BF),
             pltpu.VMEM((ROWS, W, W), F32),
             pltpu.VMEM((ROWS, 3 * W, W), BF),
             pltpu.VMEM((ROWS, W, 3 * W), BF),
+            pltpu.VMEM((ROWS, W, W), BF),
             pltpu.VMEM((ROWS, W, W), BF),
         ]
         + [pltpu.VMEM((3 * W, PH * W), F32)] * PARTS
@@ -435,10 +453,11 @@
         + [pltpu.VMEM((2, 3 * W, PH * W), BF)] * 2
         + [pltpu.VMEM((2, 8, PH * W), F32)] * 2
         + [
-            dma((len(operands),)),
+            dma((len(operands),)), dma((CHUNKS,)),
             dma((PARTS, 7)), dma((PARTS, 7)), dma((PARTS,)), dma((PARTS,)), dma((PARTS, 7)), dma((PARTS, 7)),
-            dma((PARTS, 3)), dma((PARTS, 3)), dma((CHUNKS, 4)), dma((CHUNKS, 4)),
-        ],
+            dma((3,)), dma((3,)), dma((PARTS, 3)), dma((PARTS, 3)), dma((CHUNKS, 4)), dma((CHUNKS, 4)),
+        ]
+        + [pltpu.VMEM((4, RC, W, W), BF)] * CHUNKS,
         compiler_params=pltpu.CompilerParams(
             collective_id=0, has_side_effects=True, vmem_limit_bytes=60 * 2**20
         ),

time: 61 us -> 60.6 us (level)
  no operation moved by 1% of the time
where the time goes in v4:
time: 60.6 us; the launch traced here: 60.4 us
  Pallas kernels  58.1 us (96%)
  local copies, waits for them, and re-layouts  2.31 us (4%)
    pallas_call x1, Pallas kernels, per_device(): pl.pallas_call(kernel, out_shape=jax.ShapeDtypeStruct((ROWS, W, W), BF),...  58.1 us
    unnamed x1, local copies, waits for them, and re-layouts  2.31 us

profile of v4, /device:TPU:1, one launch (start us, length us, event | category | flops | bytes accessed | tf_op | source)
XLA Modules:
  0.0 60.4 jit_solution(412154520007643389)
XLA Ops:
  0.0 58.1 %row_attention.1 = bf16[32,128,128]{2,1,0:T(8,128)(2,1)} custom-call(bf16[32,128,128]{2,1,0:T(8,128)(2,1)} %bitcast.8, s32[2,128]{1,0:T(2,128)} %bitcast.9, s32[64,64]{1,0:T(8,128)} %owner_hbm.1, f32[1,128]{1,0:T(1,128)} %bitcast.11, f32[1,128]{1,0:T(1,128)} %bitcast.12, bf16[128,128]{1,0:T(8,128)(2,1)} %wq_hbm.1, bf16[128,128]{1,0:T(8,128)(2,1)} %wk_hbm.1, ...), custom_call_target="tpu_custom_call" | custom-call | tf_op jit(solution)/shard_map/row_attention/pallas_call | solution.py:421
  58.1 2.3 %copy.14 = bf16[1,32,128,128]{3,2,1,0:T(8,128)(2,1)} copy(bf16[1,32,128,128]{3,2,1,0:T(8,128)(2,1)} %bitcast.7) | data formatting | bytes 2097152

commit v5 on v4

--- a/solution.py
+++ b/solution.py
@@ -136,8 +136,8 @@
 
     def norm_step(t, piece):
         rows, cols = [], []
-        for u in range(4):
-            i = t * 4 + u
+        for u in range(8):
+            i = t * 8 + u
             n = norm_rows(x_ref[i], gain_ref[...], offset_ref[...])
             normed[i] = n
             rows.append(n)
@@ -156,7 +156,7 @@
             c.start()
             sent.append(c)
 
-    piece = lax.fori_loop(0, ROWS // 4, norm_step, jnp.zeros((W, W), F32))
+    piece = lax.fori_loop(0, ROWS // 8, norm_step, jnp.zeros((W, W), F32))
     span = PH * ROWS
     place = lax.broadcasted_iota(I32, (KL, W), 1) // span
     for p in range(PARTS):

time: 60.6 us -> 59.8 us (0.987)
  Pallas kernels: 58.1 us -> 57.3 us
    pallas_call x1, Pallas kernels: 58.1 us -> 57.3 us  [per_device(): pl.pallas_call(kernel, out_shape=jax.ShapeDtypeStruct((ROWS, W, W), BF),...]
where the time goes in v5:
time: 59.8 us; the launch traced here: 59.6 us
  Pallas kernels  57.3 us (96%)
  local copies, waits for them, and re-layouts  2.31 us (4%)
    pallas_call x1, Pallas kernels, per_device(): pl.pallas_call(kernel, out_shape=jax.ShapeDtypeStruct((ROWS, W, W), BF),...  57.3 us
    unnamed x1, local copies, waits for them, and re-layouts  2.31 us

profile of v5, /device:TPU:1, one launch (start us, length us, event | category | flops | bytes accessed | tf_op | source)
XLA Modules:
  0.0 59.6 jit_solution(3614971367038787773)
XLA Ops:
  0.0 57.3 %row_attention.1 = bf16[32,128,128]{2,1,0:T(8,128)(2,1)} custom-call(bf16[32,128,128]{2,1,0:T(8,128)(2,1)} %bitcast.8, s32[2,128]{1,0:T(2,128)} %bitcast.9, s32[64,64]{1,0:T(8,128)} %owner_hbm.1, f32[1,128]{1,0:T(1,128)} %bitcast.11, f32[1,128]{1,0:T(1,128)} %bitcast.12, bf16[128,128]{1,0:T(8,128)(2,1)} %wq_hbm.1, bf16[128,128]{1,0:T(8,128)(2,1)} %wk_hbm.1, ...), custom_call_target="tpu_custom_call" | custom-call | tf_op jit(solution)/shard_map/row_attention/pallas_call | solution.py:421
  57.3 2.3 %copy.14 = bf16[1,32,128,128]{3,2,1,0:T(8,128)(2,1)} copy(bf16[1,32,128,128]{3,2,1,0:T(8,128)(2,1)} %bitcast.7) | data formatting | bytes 2097152
